TPU v7x, 32 devices: a whole 2x2x4 slice. The times are simulated.
32 devices in a mesh: ctx: 16 (over z, y, x), head: 2 (over core).
Axes of the slice: x: 2, y: 2, z: 4, core: 2. Of those that a mesh axis runs over, the one named last changes fastest.
Arguments:
- queries: bfloat16 [4096, 8192], P(('ctx', 'head')), may hold values from -64 to 64
- keys: bfloat16 [4096, 1024], P(('ctx', 'head')), may hold values from -64 to 64
- values: bfloat16 [4096, 1024], P(('ctx', 'head')), may hold values from -6 to 6
- doc_lengths: int32 [12], replicated, may hold values from 1 to 1024, as said below
Outputs:
- attended: bfloat16 [4096, 8192], P(('ctx', 'head'))
Inputs may be any that keep to these rules, and one draw needn't show every extreme that they name: `doc_lengths`: the lengths sum to 4096; the first document has one token, the second exactly 1024, and no other more than 1024.
All inputs are finite; a program needn't handle non-finite values.
Results may differ from a plain program's by a relative error of at most 0.004.
Values may be sent and summed in bfloat16 or wider, within the bound.
No kernel may reach another device: no remote copies, remote signals or barrier semaphores. Data moves between devices by JAX's collectives and lax.ppermute only.
A program may use at most 64 MiB of HBM per device.

v0:
```python
import jax
import jax.numpy as jnp
from jax import lax
from jax.sharding import PartitionSpec as P

H = 64
KVH = 8
HD = 128
REACH = 4


def from_behind(block, axis, distance):
    devices = range(lax.axis_size(axis))
    route = [(i - distance, i) for i in devices if i - distance in devices]
    return lax.ppermute(block, axis, route)


def doc_index(positions, doc_ends):
    return jnp.sum((doc_ends[None, :] <= positions[:, None]).astype(jnp.int32), axis=1)


def per_device(queries, keys, values, doc_lengths):
    group_size = H // KVH
    score_scale = HD ** (-0.5)
    doc_ends = jnp.cumsum(doc_lengths)
    my_span = lax.axis_index("ctx")
    local_queries, local_keys, local_values = (
        lax.all_to_all(queries, "head", split_axis=1, concat_axis=0, tiled=True),
        lax.all_to_all(keys, "head", split_axis=1, concat_axis=0, tiled=True),
        lax.all_to_all(values, "head", split_axis=1, concat_axis=0, tiled=True),
    )
    first_row = my_span * local_queries.shape[0]
    kv_own = jnp.stack((local_keys, local_values))
    span_rows = kv_own.shape[1]
    query_count = local_queries.shape[0]
    kv_heads = kv_own.shape[2] // HD
    query_rows = min(256, query_count)
    query_blocked = local_queries.reshape(query_count, kv_heads, group_size, HD)
    query_pos = first_row + jnp.arange(query_count, dtype=jnp.int32)
    query_doc = doc_index(query_pos, doc_ends)
    running = (
        jnp.full((query_count, kv_heads, group_size), -1e30, jnp.float32),
        jnp.zeros((query_count, kv_heads, group_size), jnp.float32),
        jnp.zeros((query_count, kv_heads, group_size, HD), jnp.float32),
    )

    def absorb(running, kv_pair, source):
        key_rows = kv_pair[0].reshape(span_rows, kv_heads, HD)
        value_rows = kv_pair[1].reshape(span_rows, kv_heads, HD)
        key_pos = source * span_rows + jnp.arange(span_rows, dtype=jnp.int32)
        key_doc = doc_index(key_pos, doc_ends)
        key_live = key_pos >= 0

        def one_block(block_index, current):
            allowed = (
                (query_doc[:, None] == key_doc[None, :])
                & (key_pos[None, :] <= query_pos[:, None])
                & key_live[None, :]
            )

            def update_tile(state):
                row_max, row_sum, weighted = state
                scores = (
                    jnp.einsum(
                        "qkgd,skd->qkgs",
                        query_blocked,
                        key_rows,
                        preferred_element_type=jnp.float32,
                    )
                    * score_scale
                )
                wide = allowed[:, None, None, :]
                max_new = jnp.maximum(
                    row_max, jnp.max(jnp.where(wide, scores, jnp.float32(-1e30)), axis=-1)
                )
                weights = jnp.where(wide, jnp.exp(scores - max_new[..., None]), jnp.float32(0.0))
                rescale = jnp.exp(row_max - max_new)
                sum_new = row_sum * rescale + jnp.sum(weights, axis=-1)
                acc_new = weighted * rescale[..., None] + jnp.einsum(
                    "qkgs,skd->qkgd",
                    weights.astype(jnp.bfloat16),
                    value_rows,
                    preferred_element_type=jnp.float32,
                )
                return (max_new, sum_new, acc_new)

            return lax.cond(jnp.any(allowed), update_tile, lambda state: state, current)

        return lax.fori_loop(0, query_count // query_rows, one_block, running)

    running = absorb(running, kv_own, my_span)
    for distance in range(1, REACH + 1):
        arrived = from_behind(kv_own, "ctx", distance)
        running = absorb(running, arrived, my_span - distance)
    row_max, row_sum, weighted = running
    finished = (
        (weighted / row_sum[..., None])
        .astype(jnp.bfloat16)
        .reshape(query_count, kv_heads * group_size * HD)
    )
    return lax.all_to_all(finished, "head", split_axis=0, concat_axis=1, tiled=True)


def solution(mesh):
    placed = (P(("ctx", "head"), None), P(("ctx", "head"), None), P(("ctx", "head"), None), P())
    return jax.shard_map(
        per_device, mesh=mesh, in_specs=placed, out_specs=P(("ctx", "head"), None), check_vma=False
    )
```

profile of v0, /device:TPU:8, one launch (start us, length us, event | category | flops | bytes accessed | tf_op | source)
XLA Modules:
  0.0 122.5 jit_solution(10173176610713699915)
XLA Ops:
  0.0 1.7 %copy.169 = bf16[16,2,8,512]{3,2,0,1:T(8,128)(2,1)} copy(bf16[16,2,8,512]{3,2,1,0:T(8,128)(2,1)} %bitcast.197) | data formatting | bytes 524288 | tf_op jit(solution)/shard_map/all_to_all | solution.py:30
  1.7 3.4 %all-to-all-start.2 = ((bf16[128,2,512]{2,0,1:T(8,128)(2,1)}), bf16[128,2,512]{2,0,1:T(8,128)(2,1)S(1)}, u32[]{:S(2)}, u32[]{:S(2)}) async-start(bf16[128,2,512]{2,0,1:T(8,128)(2,1)} %bitcast.171), calls=%async_computation.2 | async-start | bytes 524288 | tf_op jit(solution)/shard_map/all_to_all | solution.py:30
  5.1 1.7 %copy.170 = bf16[16,2,8,512]{3,2,0,1:T(8,128)(2,1)} copy(bf16[16,2,8,512]{3,2,1,0:T(8,128)(2,1)} %bitcast.198) | data formatting | bytes 524288 | tf_op jit(solution)/shard_map/all_to_all | solution.py:29
  6.8 3.4 %all-to-all-start = ((bf16[128,2,512]{2,0,1:T(8,128)(2,1)}), bf16[128,2,512]{2,0,1:T(8,128)(2,1)S(1)}, u32[]{:S(2)}, u32[]{:S(2)}) async-start(bf16[128,2,512]{2,0,1:T(8,128)(2,1)} %bitcast.172), calls=%async_computation | async-start | bytes 524288 | tf_op jit(solution)/shard_map/all_to_all | solution.py:29
  10.3 0.1 copy.134
  10.4 1.4 %all-to-all-done = bf16[128,2,512]{2,0,1:T(8,128)(2,1)S(1)} async-done(((bf16[128,2,512]{2,0,1:T(8,128)(2,1)}), bf16[128,2,512]{2,0,1:T(8,128)(2,1)S(1)}, u32[]{:S(2)}, u32[]{:S(2)}) %all-to-all-start) | async-done | bytes 262176 | tf_op jit(solution)/shard_map/all_to_all | solution.py:29
  11.9 0.8 pad_maximum_fusion
  12.8 3.4 %collective-permute-start = (bf16[2,256,512]{1,2,0:T(8,128)(2,1)}, bf16[2,256,512]{1,2,0:T(8,128)(2,1)}, u32[]{:S(2)}, u32[]{:S(2)}) collective-permute-start(bf16[2,256,512]{1,2,0:T(8,128)(2,1)} %pad_maximum_fusion), channel_id=1, source_target_pairs={{0,2},{2,4},{4,6},{6,8},{8,10},{10,12},{12,14},{14,16},{16,18},{18... | collective-permute-start | bytes 1572872 | tf_op jit(solution)/shard_map/ppermute | solution.py:15
  16.2 3.4 %collective-permute-start.1 = (bf16[2,256,512]{1,2,0:T(8,128)(2,1)}, bf16[2,256,512]{1,2,0:T(8,128)(2,1)}, u32[]{:S(2)}, u32[]{:S(2)}) collective-permute-start(bf16[2,256,512]{1,2,0:T(8,128)(2,1)} %pad_maximum_fusion), channel_id=1, source_target_pairs={{0,4},{2,6},{4,8},{6,10},{8,12},{10,14},{12,16},{14,18},{16,20},{1... | collective-permute-start | bytes 1572872 | tf_op jit(solution)/shard_map/ppermute | solution.py:15
  19.6 4.4 %collective-permute-start.2 = (bf16[2,256,512]{1,2,0:T(8,128)(2,1)}, bf16[2,256,512]{1,2,0:T(8,128)(2,1)}, u32[]{:S(2)}, u32[]{:S(2)}) collective-permute-start(bf16[2,256,512]{1,2,0:T(8,128)(2,1)} %pad_maximum_fusion), channel_id=1, source_target_pairs={{0,6},{2,8},{4,10},{6,12},{8,14},{10,16},{12,18},{14,20},{16,22},{... | collective-permute-start | bytes 1572872 | tf_op jit(solution)/shard_map/ppermute | solution.py:15
  24.0 3.5 %collective-permute-start.3 = (bf16[2,256,512]{1,2,0:T(8,128)(2,1)}, bf16[2,256,512]{1,2,0:T(8,128)(2,1)}, u32[]{:S(2)}, u32[]{:S(2)}) collective-permute-start(bf16[2,256,512]{1,2,0:T(8,128)(2,1)} %pad_maximum_fusion), channel_id=1, source_target_pairs={{0,8},{2,10},{4,12},{6,14},{8,16},{10,18},{12,20},{14,22},{16,24},... | collective-permute-start | bytes 1572872 | tf_op jit(solution)/shard_map/ppermute | solution.py:15
  27.5 3.1 %copy.168 = bf16[16,2,8,4096]{3,2,0,1:T(8,128)(2,1)} copy(bf16[16,2,8,4096]{3,2,1,0:T(8,128)(2,1)} %bitcast.186) | data formatting | bytes 4194304 | tf_op jit(solution)/shard_map/all_to_all | solution.py:28
  30.6 3.8 %all-to-all-start.1 = ((bf16[128,2,4096]{2,0,1:T(8,128)(2,1)}), bf16[128,2,4096]{2,0,1:T(8,128)(2,1)S(1)}, u32[]{:S(2)}, u32[]{:S(2)}) async-start(bf16[128,2,4096]{2,0,1:T(8,128)(2,1)} %bitcast.179), calls=%async_computation.1 | async-start | bytes 4194304 | tf_op jit(solution)/shard_map/all_to_all | solution.py:28
  34.4 0.2 reduce-window.8
  34.7 1.5 %and_and_fusion = (pred[256,256]{0,1:T(8,128)(4,1)S(1)}, pred[]{:T(512)}, pred[]{:T(512)}, pred[256,256]{0,1:T(8,128)(4,1)S(1)}, pred[]{:T(512)}, /*index=5*/pre...) fusion(s32[256]{0:T(256)S(1)} %iota_add_fusion.4, ...), kind=kLoop, calls=%fused_computation.106 | loop fusion | flops 1638395 | bytes 339205 | tf_op jit(solution)/shard_map/while/body/eval_jaxpr/and | solution.py:56
  39.4 1.3 %copy-done = bf16[128,2,4096]{2,0,1:T(8,128)(2,1)} copy-done((bf16[128,2,4096]{2,0,1:T(8,128)(2,1)}, bf16[128,2,4096]{2,0,1:T(8,128)(2,1)S(1)}, u32[]{:S(2)}) %copy-start) | copy-done | bytes 2097176
  40.7 2.1 %copy.138 = bf16[32,8,32,128]{3,2,1,0:T(8,128)(2,1)S(1)} copy(bf16[32,8,32,128]{3,1,2,0:T(8,128)(2,1)} %bitcast.178) | data formatting | bytes 4194304
  42.9 2.4 %broadcast_in_dim.166 = f32[256,4,8,128]{3,0,2,1:T(8,128)} broadcast(f32[]{:T(128)} %constant.103.clone.1), dimensions={} | broadcast | bytes 4194308 | tf_op jit(solution)/shard_map/broadcast_in_dim | solution.py:44
  45.3 10.6 %conditional.5 = ((f32[256,4,8]{0,2,1:T(8,128)S(1)}, f32[256,4,8]{0,2,1:T(8,128)S(1)}, f32[256,4,8,128]{3,0,2,1:T(8,128)})) conditional(s32[]{:T(128)} %convert_element_type.65, (f32[256,4,8]{0,2,1:T(8,128)S(1)}, f32[256,4,8]{0,2,1:T(8,128)S(1)}, f32[256,4,8,128]{3,0,2,1:T(8,128)}) %tuple.55, (pred[256,256]{0,1:T(8,128)(4,1)S(1)}, ...), branch_computations={%region_11.12_spmd, %region_12.0_spmd} | conditional | flops 1098924032 | bytes 36896800 | solution.py:87
  45.3 2.3 %fusion = (f32[256,4,8]{0,2,1:T(8,128)S(1)}, f32[4,256,256,8]{2,1,3,0:T(8,128)S(1)}) fusion(pred[256,256]{0,1:T(8,128)(4,1)S(1)} %get-tuple-element.317, bf16[256,4,8,128]{3,2,1,0:T(8,128)(2,1)S(1)} %get-tuple-element.473, bf16[256,4,128,1]{2,1,0,3:T(4,128)(2,1)S(1)} %bitcast.187), kind=kOutput, calls=%fused_computation.2 | convolution fusion | flops 543154176 | bytes 10846208 | tf_op jit(solution)/shard_map/while/body/eval_jaxpr/cond/branch_1_fun/qkgd,skd->qkgs/dot_general | solution.py:64
  47.7 1.8 %fusion.4 = f32[256,4,8]{0,2,1:T(8,128)S(1)} fusion(f32[4,256,256,8]{2,1,3,0:T(8,128)S(1)} %get-tuple-element.528, f32[256,4,8]{0,2,1:T(8,128)S(1)} %max.11, pred[256,256]{0,1:T(8,128)(4,1)S(1)} %get-tuple-element.317), kind=kLoop, calls=%fused_computation.6 | loop fusion | flops 8380416 | bytes 8519680 | tf_op jit(solution)/shard_map/while/body/eval_jaxpr/cond/branch_1_fun/reduce_sum | solution.py:78
  49.5 6.4 %bitcast_add_fusion = f32[256,4,8,128]{3,0,2,1:T(8,128)} fusion(f32[256,4,8,128]{3,0,2,1:T(8,128)} %get-tuple-element.321, f32[256,4,8]{0,2,1:T(8,128)S(1)} %get-tuple-element.510, f32[4,256,256,8]{2,1,3,0:T(8,128)S(1)} %get-tuple-element.528, f32[256,4,8]{0,2,1:T(8,128)S(1)} %max.11, pred[256,256]{0,1:T(8,128)(4,1)S(1)} %get-tuple-element.317, ...), kind=kOutput, calls=%fused_computation.8 | convolution fusion | flops 547356672 | bytes 17170432 | tf_op jit(solution)/shard_map/while/body/eval_jaxpr/cond/branch_1_fun/qkgs,skd->qkgd/dot_general | solution.py:79
  56.0 1.1 fusion.99
  57.0 10.8 %conditional.6 = ((f32[256,4,8]{0,2,1:T(8,128)S(1)}, f32[256,4,8]{0,2,1:T(8,128)S(1)}, f32[256,4,8,128]{3,0,2,1:T(8,128)})) conditional(s32[]{:T(128)} %convert_element_type.64, (f32[256,4,8]{0,2,1:T(8,128)S(1)}, f32[256,4,8]{0,2,1:T(8,128)S(1)}, f32[256,4,8,128]{3,0,2,1:T(8,128)}) %get-tuple-element.591, (pred[256,256]{0,1:T(8,128)(4,1)S(1)}, ...), branch_computations={%region_15.16_spmd, %region_16.19_spmd} | conditional | flops 1098924032 | bytes 36896800 | solution.py:87
  57.2 2.4 %fusion.19 = (f32[256,4,8]{0,2,1:T(8,128)S(1)}, f32[4,256,256,8]{2,1,3,0:T(8,128)S(1)}) fusion(pred[256,256]{0,1:T(8,128)(4,1)S(1)} %get-tuple-element.324, bf16[256,4,8,128]{3,2,1,0:T(8,128)(2,1)S(1)} %get-tuple-element.480, bf16[256,4,128]{0,2,1:T(8,128)(2,1)S(1)} %get-tuple-element.479), kind=kOutput, calls=%fused_computation.23 | convolution fusion | flops 543154176 | bytes 10846208 | tf_op jit(solution)/shard_map/while/body/eval_jaxpr/cond/branch_1_fun/qkgd,skd->qkgs/dot_general | solution.py:64
  59.6 1.8 %fusion.23 = f32[256,4,8]{0,2,1:T(8,128)S(1)} fusion(f32[4,256,256,8]{2,1,3,0:T(8,128)S(1)} %get-tuple-element.530, f32[256,4,8]{0,2,1:T(8,128)S(1)} %max.12, pred[256,256]{0,1:T(8,128)(4,1)S(1)} %get-tuple-element.324), kind=kLoop, calls=%fused_computation.27 | loop fusion | flops 8380416 | bytes 8519680 | tf_op jit(solution)/shard_map/while/body/eval_jaxpr/cond/branch_1_fun/reduce_sum | solution.py:78
  61.5 6.4 %bitcast_add_fusion.1 = f32[256,4,8,128]{3,0,2,1:T(8,128)} fusion(f32[256,4,8,128]{3,0,2,1:T(8,128)} %get-tuple-element.340, f32[256,4,8]{0,2,1:T(8,128)S(1)} %get-tuple-element.512, f32[4,256,256,8]{2,1,3,0:T(8,128)S(1)} %get-tuple-element.530, f32[256,4,8]{0,2,1:T(8,128)S(1)} %max.12, pred[256,256]{0,1:T(8,128)(4,1)S(1)} %get-tuple-element.324, ...), kind=kOutput, calls=%fused_computation.29 | convolution fusion | flops 547356672 | bytes 17170432 | tf_op jit(solution)/shard_map/while/body/eval_jaxpr/cond/branch_1_fun/qkgs,skd->qkgd/dot_general | solution.py:79
  67.8 1.1 fusion.98
  68.9 10.6 %conditional.7 = ((f32[256,4,8]{0,2,1:T(8,128)S(1)}, f32[256,4,8]{0,2,1:T(8,128)S(1)}, f32[256,4,8,128]{3,0,2,1:T(8,128)})) conditional(s32[]{:T(128)} %convert_element_type.62, (f32[256,4,8]{0,2,1:T(8,128)S(1)}, f32[256,4,8]{0,2,1:T(8,128)S(1)}, f32[256,4,8,128]{3,0,2,1:T(8,128)}) %get-tuple-element.592, (pred[256,256]{0,1:T(8,128)(4,1)S(1)}, ...), branch_computations={%region_19.20_spmd, %region_20.0_spmd} | conditional | flops 1098924032 | bytes 36896800 | solution.py:87
  68.9 2.4 %fusion.38 = (f32[256,4,8]{0,2,1:T(8,128)S(1)}, f32[4,256,256,8]{2,1,3,0:T(8,128)S(1)}) fusion(pred[256,256]{0,1:T(8,128)(4,1)S(1)} %get-tuple-element.345, bf16[256,4,8,128]{3,2,1,0:T(8,128)(2,1)S(1)} %get-tuple-element.487, bf16[256,4,128]{0,2,1:T(8,128)(2,1)S(1)} %get-tuple-element.486), kind=kOutput, calls=%fused_computation.44 | convolution fusion | flops 543154176 | bytes 10846208 | tf_op jit(solution)/shard_map/while/body/eval_jaxpr/cond/branch_1_fun/qkgd,skd->qkgs/dot_general | solution.py:64
  71.3 1.8 %fusion.42 = f32[256,4,8]{0,2,1:T(8,128)S(1)} fusion(f32[4,256,256,8]{2,1,3,0:T(8,128)S(1)} %get-tuple-element.532, f32[256,4,8]{0,2,1:T(8,128)S(1)} %max.13, pred[256,256]{0,1:T(8,128)(4,1)S(1)} %get-tuple-element.345), kind=kLoop, calls=%fused_computation.48 | loop fusion | flops 8380416 | bytes 8519680 | tf_op jit(solution)/shard_map/while/body/eval_jaxpr/cond/branch_1_fun/reduce_sum | solution.py:78
  73.2 6.4 %bitcast_add_fusion.2 = f32[256,4,8,128]{3,0,2,1:T(8,128)} fusion(f32[256,4,8,128]{3,0,2,1:T(8,128)} %get-tuple-element.349, f32[256,4,8]{0,2,1:T(8,128)S(1)} %get-tuple-element.514, f32[4,256,256,8]{2,1,3,0:T(8,128)S(1)} %get-tuple-element.532, f32[256,4,8]{0,2,1:T(8,128)S(1)} %max.13, pred[256,256]{0,1:T(8,128)(4,1)S(1)} %get-tuple-element.345, ...), kind=kOutput, calls=%fused_computation.50 | convolution fusion | flops 547356672 | bytes 17170432 | tf_op jit(solution)/shard_map/while/body/eval_jaxpr/cond/branch_1_fun/qkgs,skd->qkgd/dot_general | solution.py:79
  79.6 11.7 %conditional.8 = ((f32[256,4,8]{0,2,1:T(8,128)S(1)}, f32[256,4,8]{0,2,1:T(8,128)S(1)}, f32[256,4,8,128]{3,0,2,1:T(8,128)})) conditional(s32[]{:T(128)} %convert_element_type.60, (f32[256,4,8]{0,2,1:T(8,128)S(1)}, f32[256,4,8]{0,2,1:T(8,128)S(1)}, f32[256,4,8,128]{3,0,2,1:T(8,128)}) %get-tuple-element.593, (pred[256,256]{0,1:T(8,128)(4,1)S(1)}, ...), branch_computations={%region_23.24_spmd, %region_24.27_spmd} | conditional | flops 1098924032 | bytes 37945376 | solution.py:87
  79.6 1.1 fusion.96
  80.6 2.3 %fusion.57 = (f32[256,4,8]{0,2,1:T(8,128)S(1)}, f32[4,256,256,8]{2,1,3,0:T(8,128)S(1)}) fusion(pred[256,256]{0,1:T(8,128)(4,1)S(1)} %get-tuple-element.352, bf16[256,4,128,1]{0,2,3,1:T(8,128)(2,1)S(1)} %bitcast.195, bf16[256,4,8,128]{3,2,1,0:T(8,128)(2,1)S(1)} %get-tuple-element.494), kind=kOutput, calls=%fused_computation.65 | convolution fusion | flops 543154176 | bytes 10846208 | tf_op jit(solution)/shard_map/while/body/eval_jaxpr/cond/branch_1_fun/qkgd,skd->qkgs/dot_general | solution.py:64
  83.0 1.8 %fusion.61 = f32[256,4,8]{0,2,1:T(8,128)S(1)} fusion(f32[4,256,256,8]{2,1,3,0:T(8,128)S(1)} %get-tuple-element.536, f32[256,4,8]{0,2,1:T(8,128)S(1)} %max.14, pred[256,256]{0,1:T(8,128)(4,1)S(1)} %get-tuple-element.352), kind=kLoop, calls=%fused_computation.69 | loop fusion | flops 8380416 | bytes 8519680 | tf_op jit(solution)/shard_map/while/body/eval_jaxpr/cond/branch_1_fun/reduce_sum | solution.py:78
  84.8 6.4 %bitcast_add_fusion.3 = f32[256,4,8,128]{3,0,2,1:T(8,128)} fusion(f32[256,4,8,128]{3,0,2,1:T(8,128)} %get-tuple-element.356, f32[256,4,8]{0,2,1:T(8,128)S(1)} %get-tuple-element.516, bf16[256,4,128,1]{0,2,3,1:T(8,128)(2,1)S(1)} %bitcast.191, f32[4,256,256,8]{2,1,3,0:T(8,128)S(1)} %get-tuple-element.536, f32[256,4,8]{0,2,1:T(8,128)S(1)} %max.14, ...), kind=kOutput, calls=%fused_computation.71 | convolution fusion | flops 547356672 | bytes 17170432 | tf_op jit(solution)/shard_map/while/body/eval_jaxpr/cond/branch_1_fun/qkgs,skd->qkgd/dot_general | solution.py:79
  91.2 11.6 %conditional.9 = ((f32[256,4,8]{0,2,1:T(8,128)S(1)}, f32[256,4,8,128]{3,0,2,1:T(8,128)})) conditional(s32[]{:T(128)} %convert_element_type.58, (f32[256,4,8]{0,2,1:T(8,128)S(1)}, f32[256,4,8,128]{3,0,2,1:T(8,128)}) %tuple.60, (pred[256,256]{0,1:T(8,128)(4,1)S(1)}, bf16[2,256,512]{1,2,0:T(8,128)(2,1)}, bf16[256,4,8,128]{3,2,1,0:T(8,128)(2,1)S(1)}, ...), branch_computations={%region_27.28_spmd, %region_28.0_spmd} | conditional | flops 1098924032 | bytes 37879832 | solution.py:87
  91.2 1.1 fusion.97
  92.3 2.3 %fusion.74 = (f32[256,4,8]{0,2,1:T(8,128)S(1)}, f32[4,256,256,8]{2,1,3,0:T(8,128)S(1)}) fusion(pred[256,256]{0,1:T(8,128)(4,1)S(1)} %get-tuple-element.359, bf16[256,4,128,1]{0,2,3,1:T(8,128)(2,1)S(1)} %bitcast.196, bf16[256,4,8,128]{3,2,1,0:T(8,128)(2,1)S(1)} %get-tuple-element.500), kind=kOutput, calls=%fused_computation.84 | convolution fusion | flops 543154176 | bytes 10846208 | tf_op jit(solution)/shard_map/while/body/eval_jaxpr/cond/branch_1_fun/qkgd,skd->qkgs/dot_general | solution.py:64
  94.7 1.8 %fusion.78 = f32[256,4,8]{0,2,1:T(8,128)S(1)} fusion(f32[4,256,256,8]{2,1,3,0:T(8,128)S(1)} %get-tuple-element.540, f32[256,4,8]{0,2,1:T(8,128)S(1)} %max.15, pred[256,256]{0,1:T(8,128)(4,1)S(1)} %get-tuple-element.359), kind=kLoop, calls=%fused_computation.88 | loop fusion | flops 8380416 | bytes 8519680 | tf_op jit(solution)/shard_map/while/body/eval_jaxpr/cond/branch_1_fun/reduce_sum | solution.py:78
  96.5 6.4 %bitcast_add_fusion.4 = f32[256,4,8,128]{3,0,2,1:T(8,128)} fusion(f32[256,4,8,128]{3,0,2,1:T(8,128)} %get-tuple-element.362, f32[256,4,8]{0,2,1:T(8,128)S(1)} %get-tuple-element.518, bf16[256,4,128,1]{0,2,3,1:T(8,128)(2,1)S(1)} %bitcast.192, f32[4,256,256,8]{2,1,3,0:T(8,128)S(1)} %get-tuple-element.540, f32[256,4,8]{0,2,1:T(8,128)S(1)} %max.15, ...), kind=kOutput, calls=%fused_computation.90 | convolution fusion | flops 547356672 | bytes 17170432 | tf_op jit(solution)/shard_map/while/body/eval_jaxpr/cond/branch_1_fun/qkgs,skd->qkgd/dot_general | solution.py:79
  102.9 2.9 %divide_convert_fusion = bf16[256,4,8,128]{3,0,2,1:T(8,128)(2,1)S(1)} fusion(f32[256,4,8,128]{3,0,2,1:T(8,128)} %get-tuple-element.389, f32[256,4,8]{0,2,1:T(8,128)S(1)} %get-tuple-element.390), kind=kLoop, calls=%fused_computation.101 | loop fusion | flops 2097152 | bytes 6324224 | tf_op jit(solution)/shard_map/convert_element_type | solution.py:98
  105.7 1.4 %copy.95 = bf16[256,4,8,128]{3,2,1,0:T(8,128)(2,1)S(1)} copy(bf16[256,4,8,128]{3,0,2,1:T(8,128)(2,1)S(1)} %divide_convert_fusion) | data formatting | bytes 4194304 | tf_op jit(solution)/shard_map/convert_element_type | solution.py:98
  107.1 2.3 %all_to_all.59 = bf16[2,128,4096]{2,1,0:T(8,128)(2,1)} reshape(bf16[256,4,8,128]{3,2,1,0:T(8,128)(2,1)S(1)} %copy.95) | data formatting | bytes 4194304 | tf_op jit(solution)/shard_map/all_to_all | solution.py:101
  109.4 6.6 %all_to_all.67 = bf16[2,128,4096]{2,1,0:T(8,128)(2,1)S(1)} all-to-all(bf16[2,128,4096]{2,1,0:T(8,128)(2,1)} %all_to_all.59), channel_id=1, replica_groups=mesh['ctx'=16,'head'=2] {'head'}, dimensions={0} | all-to-all | bytes 4194304 | tf_op jit(solution)/shard_map/all_to_all | solution.py:101
  116.0 2.5 %copy.96 = bf16[128,2,4096]{0,2,1:T(8,128)(2,1)} copy(bf16[128,2,4096]{2,0,1:T(8,128)(2,1)S(1)} %bitcast.180) | data formatting | bytes 4194304 | tf_op jit(solution)/shard_map/all_to_all | solution.py:101
  118.5 4.1 %copy.97 = bf16[128,8192]{1,0:T(8,128)(2,1)} copy(bf16[128,8192]{0,1:T(8,128)(2,1)} %bitcast.181) | data formatting | bytes 4194304 | tf_op jit(solution)/shard_map/all_to_all | solution.py:101
  (35 shorter events, 0.6 us)
Async XLA Ops:
  0.0 34.4 %copy-start.1 = (s32[12]{0:T(128)S(1)}, s32[12]{0:T(128)}, u32[]{:S(2)}) copy-start(s32[12]{0:T(128)} %param.17) | copy-start | bytes 148
  1.7 5.1 %all-to-all-start.2 = ((bf16[128,2,512]{2,0,1:T(8,128)(2,1)}), bf16[128,2,512]{2,0,1:T(8,128)(2,1)S(1)}, u32[]{:S(2)}, u32[]{:S(2)}) async-start(bf16[128,2,512]{2,0,1:T(8,128)(2,1)} %bitcast.171), calls=%async_computation.2 | async-start | bytes 524288 | tf_op jit(solution)/shard_map/all_to_all | solution.py:30
  6.8 5.0 %all-to-all-start = ((bf16[128,2,512]{2,0,1:T(8,128)(2,1)}), bf16[128,2,512]{2,0,1:T(8,128)(2,1)S(1)}, u32[]{:S(2)}, u32[]{:S(2)}) async-start(bf16[128,2,512]{2,0,1:T(8,128)(2,1)} %bitcast.172), calls=%async_computation | async-start | bytes 524288 | tf_op jit(solution)/shard_map/all_to_all | solution.py:29
  12.8 43.2 %collective-permute-start = (bf16[2,256,512]{1,2,0:T(8,128)(2,1)}, bf16[2,256,512]{1,2,0:T(8,128)(2,1)}, u32[]{:S(2)}, u32[]{:S(2)}) collective-permute-start(bf16[2,256,512]{1,2,0:T(8,128)(2,1)} %pad_maximum_fusion), channel_id=1, source_target_pairs={{0,2},{2,4},{4,6},{6,8},{8,10},{10,12},{12,14},{14,16},{16,18},{18... | collective-permute-start | bytes 1572872 | tf_op jit(solution)/shard_map/ppermute | solution.py:15
  16.2 51.7 %collective-permute-start.1 = (bf16[2,256,512]{1,2,0:T(8,128)(2,1)}, bf16[2,256,512]{1,2,0:T(8,128)(2,1)}, u32[]{:S(2)}, u32[]{:S(2)}) collective-permute-start(bf16[2,256,512]{1,2,0:T(8,128)(2,1)} %pad_maximum_fusion), channel_id=1, source_target_pairs={{0,4},{2,6},{4,8},{6,10},{8,12},{10,14},{12,16},{14,18},{16,20},{1... | collective-permute-start | bytes 1572872 | tf_op jit(solution)/shard_map/ppermute | solution.py:15
  19.6 60.0 %collective-permute-start.2 = (bf16[2,256,512]{1,2,0:T(8,128)(2,1)}, bf16[2,256,512]{1,2,0:T(8,128)(2,1)}, u32[]{:S(2)}, u32[]{:S(2)}) collective-permute-start(bf16[2,256,512]{1,2,0:T(8,128)(2,1)} %pad_maximum_fusion), channel_id=1, source_target_pairs={{0,6},{2,8},{4,10},{6,12},{8,14},{10,16},{12,18},{14,20},{16,22},{... | collective-permute-start | bytes 1572872 | tf_op jit(solution)/shard_map/ppermute | solution.py:15
  24.0 67.3 %collective-permute-start.3 = (bf16[2,256,512]{1,2,0:T(8,128)(2,1)}, bf16[2,256,512]{1,2,0:T(8,128)(2,1)}, u32[]{:S(2)}, u32[]{:S(2)}) collective-permute-start(bf16[2,256,512]{1,2,0:T(8,128)(2,1)} %pad_maximum_fusion), channel_id=1, source_target_pairs={{0,8},{2,10},{4,12},{6,14},{8,16},{10,18},{12,20},{14,22},{16,24},... | collective-permute-start | bytes 1572872 | tf_op jit(solution)/shard_map/ppermute | solution.py:15
  30.6 8.8 %all-to-all-start.1 = ((bf16[128,2,4096]{2,0,1:T(8,128)(2,1)}), bf16[128,2,4096]{2,0,1:T(8,128)(2,1)S(1)}, u32[]{:S(2)}, u32[]{:S(2)}) async-start(bf16[128,2,4096]{2,0,1:T(8,128)(2,1)} %bitcast.179), calls=%async_computation.1 | async-start | bytes 4194304 | tf_op jit(solution)/shard_map/all_to_all | solution.py:28
  39.4 1.3 %copy-start = (bf16[128,2,4096]{2,0,1:T(8,128)(2,1)}, bf16[128,2,4096]{2,0,1:T(8,128)(2,1)S(1)}, u32[]{:S(2)}) copy-start(bf16[128,2,4096]{2,0,1:T(8,128)(2,1)S(1)} %all-to-all-done.1) | copy-start | bytes 6291460
where the time goes:
time: 124 us; the launch traced here: 123 us
  matrix products  43.7 us (35%)
  local copies, waits for them, and re-layouts  27.1 us (22%)
  starting transfers between devices  25.3 us (20%)
  other arithmetic  14.7 us (12%)
  blocking collectives  6.61 us (5%)
  between operations  3.33 us (3%)
  waiting for transfers between devices  1.42 us (1%)
    dot_general x5, matrix products, update_tile(): jnp.einsum('qkgs,skd->qkgd', weights.astype(jnp.bfloat16), value_rows, pr...  31.9 us
    ppermute x4, starting transfers between devices, from_behind(): return lax.ppermute(block, axis, route)  14.7 us
    dot_general x5, matrix products, update_tile(): jnp.einsum('qkgd,skd->qkgs', query_blocked, key_rows, preferred_element_t...  11.7 us
    reduce_sum x5, other arithmetic, update_tile(): sum_new = row_sum * rescale + jnp.sum(weights, axis=-1)  9.07 us
    all_to_all x3, local copies, waits for them, and re-layouts, per_device(): lax.all_to_all(finished, 'head', split_axis=0, concat_axis=1, tiled=True)  8.82 us
    all_to_all x1, blocking collectives, per_device(): lax.all_to_all(finished, 'head', split_axis=0, concat_axis=1, tiled=True)  6.61 us
    slice x4, local copies, waits for them, and re-layouts, absorb(): value_rows = kv_pair[1].reshape(span_rows, kv_heads, HD)  4.26 us
    all_to_all x1, starting transfers between devices, per_device(): lax.all_to_all(queries, 'head', split_axis=1, concat_axis=0, tiled=True)  3.76 us
  transfers between devices with their start and end apart: 7, of which 1 were waited for; matrix products, arithmetic and copies ran while one was open for 46% of the time, Pallas kernels for 0%

commit v1 on v0

v1 whole, which is shorter than its diff:
```python
import functools
import math

import jax
import jax.numpy as jnp
from jax import lax
from jax.experimental import pallas as pl
from jax.experimental.pallas import tpu as pltpu
from jax.sharding import PartitionSpec as P

HD = 128
REACH = 4
NEVER = -1e30


def from_behind(block, axis, distance):
    devices = range(lax.axis_size(axis))
    route = [(i - distance, i) for i in devices if i - distance in devices]
    return lax.ppermute(block, axis, route)


def attend_kernel(place_ref, lengths_ref, q_ref, *refs, group_size, heads_per_chunk):
    kv_refs, (out_ref, lo_ref, max_ref, acc_ref) = refs[:-4], refs[-4:]
    rows = q_ref.shape[0]
    span_rows = kv_refs[0].shape[0]
    chunk_rows = heads_per_chunk * rows
    first_query = place_ref[0]
    half = place_ref[1]
    own_start = first_query - half * rows
    score_scale = HD ** (-0.5) * math.log2(math.e)

    @pl.when(pl.program_id(0) == 0)
    def _():
        pos = first_query + lax.broadcasted_iota(jnp.int32, (rows, HD), 0)

        def later_doc(i, carry):
            start, lo = carry
            start = start + lengths_ref[i]
            return start, jnp.where(start <= pos, start, lo)

        _, lo = lax.fori_loop(
            0, lengths_ref.shape[0], later_doc, (jnp.int32(0), jnp.zeros((rows, HD), jnp.int32))
        )
        lo_ref[...] = lo

    def first_doc(i, carry):
        start, lo = carry
        start = start + lengths_ref[i]
        return start, jnp.where(start <= first_query, start, lo)

    _, lo_first = lax.fori_loop(0, lengths_ref.shape[0], first_doc, (jnp.int32(0), jnp.int32(0)))

    def absorb(key_block, value_block, key_start, causal, initial):
        keys = key_block.shape[0]
        key_pos = key_start + lax.broadcasted_iota(jnp.int32, (rows, keys), 1)
        lo = jnp.concatenate([lo_ref[...]] * (keys // HD), axis=1)
        allowed = key_pos >= lo
        if causal:
            query_pos = first_query + lax.broadcasted_iota(jnp.int32, (rows, keys), 0)
            allowed = allowed & (key_pos <= query_pos)
        allowed = jnp.concatenate([allowed] * heads_per_chunk, axis=0)
        widened = jnp.concatenate([value_block, jnp.ones_like(value_block)], axis=1)
        for chunk in range(group_size // heads_per_chunk):
            at = pl.ds(chunk * chunk_rows, chunk_rows)
            q = jnp.concatenate(
                [
                    q_ref[:, (chunk * heads_per_chunk + h) * HD : (chunk * heads_per_chunk + h + 1) * HD]
                    for h in range(heads_per_chunk)
                ],
                axis=0,
            )
            scores = lax.dot_general(
                q, key_block, (((1,), (1,)), ((), ())), preferred_element_type=jnp.float32
            )
            scores = jnp.where(allowed, scores * score_scale, NEVER)
            block_max = jnp.max(scores, axis=1, keepdims=True)
            if initial:
                max_new = block_max
            else:
                max_old = max_ref[at, :]
                max_new = jnp.maximum(max_old, block_max)
            weights = jnp.exp2(scores - max_new[:, :1]).astype(jnp.bfloat16)
            added = jnp.dot(weights, widened, preferred_element_type=jnp.float32)
            if initial:
                acc_ref[at, :] = added
                max_ref[at, :] = jnp.broadcast_to(max_new, (chunk_rows, HD))
            else:
                rescale = jnp.exp2(max_old - max_new)
                acc_ref[at, :] = acc_ref[at, :] * jnp.concatenate([rescale] * 2, axis=1) + added
                max_ref[at, :] = max_new

    mine = pl.ds(pl.multiple_of(half * rows, rows), rows)
    absorb(kv_refs[0][mine, :], kv_refs[1][mine, :], first_query, True, True)

    @pl.when((half == 1) & (own_start + rows > lo_first))
    def _():
        absorb(kv_refs[0][:rows, :], kv_refs[1][:rows, :], own_start, False, False)

    for distance in range(1, len(kv_refs) // 2):
        start = own_start - distance * span_rows

        @pl.when(start + span_rows > lo_first)
        def _():
            absorb(kv_refs[2 * distance][...], kv_refs[2 * distance + 1][...], start, False, False)

    for h in range(group_size):
        acc = acc_ref[h * rows : (h + 1) * rows, :]
        out_ref[:, h * HD : (h + 1) * HD] = (acc[:, :HD] / acc[:, HD:]).astype(jnp.bfloat16)


def per_device(queries, keys, values, doc_lengths):
    rows = queries.shape[0]
    kv_heads = keys.shape[1] // HD
    group_size = queries.shape[1] // keys.shape[1]
    half = lax.axis_index("head")
    span = lax.axis_index("ctx")
    place = jnp.stack([(span * lax.axis_size("head") + half) * rows, half]).astype(jnp.int32)

    own = jnp.concatenate([keys, values], axis=1)
    arrived = [own] + [from_behind(own, "ctx", d) for d in range(1, REACH + 1)]
    spans = [lax.all_gather(block, "head", axis=0, tiled=True) for block in arrived]

    smem = pl.BlockSpec(memory_space=pltpu.SMEM)
    kv_specs, kv_args = [], []
    for block in spans:
        kv_specs.append(pl.BlockSpec((block.shape[0], HD), lambda g: (0, g)))
        kv_specs.append(pl.BlockSpec((block.shape[0], HD), lambda g: (0, kv_heads + g)))
        kv_args += [block, block]
    head_rows = group_size * rows
    return pl.pallas_call(
        functools.partial(attend_kernel, group_size=group_size, heads_per_chunk=2),
        grid=(kv_heads,),
        in_specs=[smem, smem, pl.BlockSpec((rows, group_size * HD), lambda g: (0, g))] + kv_specs,
        out_specs=pl.BlockSpec((rows, group_size * HD), lambda g: (0, g)),
        out_shape=jax.ShapeDtypeStruct(queries.shape, queries.dtype),
        scratch_shapes=[
            pltpu.VMEM((rows, HD), jnp.int32),
            pltpu.VMEM((head_rows, HD), jnp.float32),
            pltpu.VMEM((head_rows, 2 * HD), jnp.float32),
        ],
        compiler_params=pltpu.CompilerParams(
            dimension_semantics=("arbitrary",), vmem_limit_bytes=32 * 1024 * 1024
        ),
        name="attend",
    )(place, doc_lengths, queries, *kv_args)


def solution(mesh):
    placed = P(("ctx", "head"), None)
    return jax.shard_map(
        per_device, mesh=mesh, in_specs=(placed, placed, placed, P()), out_specs=placed, check_vma=False
    )
```

time: 124 us -> 136 us (1.097)
  waiting for transfers between devices: 1.42 us -> 54.4 us
  matrix products: 43.7 us -> 0 us
  Pallas kernels: 0 us -> 38.5 us
  local copies, waits for them, and re-layouts: 27.1 us -> 12.2 us
  other arithmetic: 14.7 us -> 0.08 us
  between operations: 3.33 us -> 13.2 us
  starting transfers between devices: 25.3 us -> 15.7 us
  blocking collectives: 6.61 us -> 0 us
    ppermute x4, waiting for transfers between devices: 0.01 us -> 45.7 us  [from_behind(): return lax.ppermute(block, axis, route)]
    dot_general x10 -> x0, matrix products: 43.7 us -> none  [the longest x5 31.9 us: update_tile(): jnp.einsum('qkgs,skd->qkgd', weights.astype(jnp.bfloat16), value_rows, pr...]
    pallas_call x0 -> x1, Pallas kernels: none -> 38.5 us  [per_device(): pl.pallas_call(functools.partial(attend_kernel, group_size=group_size, he...]
    all_to_all x6 -> x0, local copies, waits for them, and re-layouts: 15.3 us -> none  [the longest x3 8.82 us: per_device(): lax.all_to_all(finished, 'head', split_axis=0, concat_axis=1, tiled=True)]
    all_to_all x3 -> x0, starting transfers between devices: 10.7 us -> none  [the longest x1 3.76 us: per_device(): lax.all_to_all(queries, 'head', split_axis=1, concat_axis=0, tiled=True)]
    reduce_sum x6 -> x0, other arithmetic: 9.17 us -> none  [the longest x5 9.07 us: update_tile(): sum_new = row_sum * rescale + jnp.sum(weights, axis=-1)]
    all_gather x0 -> x5, waiting for transfers between devices: none -> 8.65 us  [per_device(): lax.all_gather(block, 'head', axis=0, tiled=True)]
    unnamed x5 -> x25, local copies, waits for them, and re-layouts: 3.38 us -> 11.2 us
  transfers between devices with their start and end apart: 7 -> 9, of which waited for: 1 -> 5; matrix products, arithmetic and copies ran while one was open for 46% -> 0% of each run, Pallas kernels for 0% -> 0%
where the time goes in v1:
time: 136 us; the launch traced here: 134 us
  waiting for transfers between devices  54.4 us (40%)
  Pallas kernels  38.5 us (28%)
  starting transfers between devices  15.7 us (12%)
  between operations  13.2 us (10%)
  local copies, waits for them, and re-layouts  12.2 us (9%)
    ppermute x4, waiting for transfers between devices, from_behind(): return lax.ppermute(block, axis, route)  45.7 us
    pallas_call x1, Pallas kernels, per_device(): pl.pallas_call(functools.partial(attend_kernel, group_size=group_size, he...  38.5 us
    ppermute x4, starting transfers between devices, from_behind(): return lax.ppermute(block, axis, route)  15.6 us
    unnamed x25, local copies, waits for them, and re-layouts  11.2 us
    all_gather x5, waiting for transfers between devices, per_device(): lax.all_gather(block, 'head', axis=0, tiled=True)  8.65 us
  transfers between devices with their start and end apart: 9, of which 5 were waited for; matrix products, arithmetic and copies ran while one was open for 0% of the time, Pallas kernels for 0%

profile of v1, /device:TPU:8, one launch (start us, length us, event | category | flops | bytes accessed | tf_op | source)
XLA Modules:
  0.0 134.2 jit_solution(8362496133432404692)
XLA Ops:
  6.5 0.0 copy-start.6
  6.5 0.0 copy-start.5
  6.5 0.0 all-gather.6.cloned.1.call-start
  6.5 1.1 constant_dynamic-update-slice_fusion.1
  7.7 1.0 constant_dynamic-update-slice_fusion
  8.6 0.0 copy-start.7
  8.6 0.8 copy-done.7
  9.4 0.0 all-gather.6.cloned.1.call-update
  9.5 0.0 all-gather.14.cloned.1.call-start
  9.5 3.5 %collective-permute-start.3 = (bf16[128,2048]{1,0:T(8,128)(2,1)}, bf16[128,2048]{1,0:T(8,128)(2,1)S(1)}, u32[]{:S(2)}, u32[]{:S(2)}) collective-permute-start(bf16[128,2048]{1,0:T(8,128)(2,1)} %copy-done.7), channel_id=1, source_target_pairs={{0,8},{2,10},{4,12},{6,14},{8,16},{10,18},{12,20},{14,22},{16,24},... | collective-permute-start | bytes 1572872 | tf_op jit(solution)/shard_map/ppermute | solution.py:19
  13.0 12.3 %collective-permute-done.3 = bf16[128,2048]{1,0:T(8,128)(2,1)S(1)} collective-permute-done((bf16[128,2048]{1,0:T(8,128)(2,1)}, bf16[128,2048]{1,0:T(8,128)(2,1)S(1)}, u32[]{:S(2)}, u32[]{:S(2)}) %collective-permute-start.3) | collective-permute-done | bytes 524320 | tf_op jit(solution)/shard_map/ppermute | solution.py:19
  25.3 0.0 copy-start.8
  25.3 0.8 copy-done.8
  26.1 0.0 all-gather.14.cloned.1.call-update
  26.1 0.0 all-gather.12.cloned.1.call-start
  26.1 4.4 %collective-permute-start.2 = (bf16[128,2048]{1,0:T(8,128)(2,1)}, bf16[128,2048]{1,0:T(8,128)(2,1)S(1)}, u32[]{:S(2)}, u32[]{:S(2)}) collective-permute-start(bf16[128,2048]{1,0:T(8,128)(2,1)} %copy-done.7), channel_id=1, source_target_pairs={{0,6},{2,8},{4,10},{6,12},{8,14},{10,16},{12,18},{14,20},{16,22},{... | collective-permute-start | bytes 1572872 | tf_op jit(solution)/shard_map/ppermute | solution.py:19
  30.5 11.4 %collective-permute-done.2 = bf16[128,2048]{1,0:T(8,128)(2,1)S(1)} collective-permute-done((bf16[128,2048]{1,0:T(8,128)(2,1)}, bf16[128,2048]{1,0:T(8,128)(2,1)S(1)}, u32[]{:S(2)}, u32[]{:S(2)}) %collective-permute-start.2) | collective-permute-done | bytes 524320 | tf_op jit(solution)/shard_map/ppermute | solution.py:19
  41.9 0.0 copy-start.9
  41.9 0.8 copy-done.9
  42.7 0.0 all-gather.12.cloned.1.call-update
  42.8 0.0 all-gather.10.cloned.1.call-start
  42.8 3.4 %collective-permute-start.1 = (bf16[128,2048]{1,0:T(8,128)(2,1)}, bf16[128,2048]{1,0:T(8,128)(2,1)S(1)}, u32[]{:S(2)}, u32[]{:S(2)}) collective-permute-start(bf16[128,2048]{1,0:T(8,128)(2,1)} %copy-done.7), channel_id=1, source_target_pairs={{0,4},{2,6},{4,8},{6,10},{8,12},{10,14},{12,16},{14,18},{16,20},{1... | collective-permute-start | bytes 1572872 | tf_op jit(solution)/shard_map/ppermute | solution.py:19
  46.3 11.4 %collective-permute-done.1 = bf16[128,2048]{1,0:T(8,128)(2,1)S(1)} collective-permute-done((bf16[128,2048]{1,0:T(8,128)(2,1)}, bf16[128,2048]{1,0:T(8,128)(2,1)S(1)}, u32[]{:S(2)}, u32[]{:S(2)}) %collective-permute-start.1) | collective-permute-done | bytes 524320 | tf_op jit(solution)/shard_map/ppermute | solution.py:19
  57.7 0.0 copy-start.10
  57.7 0.8 copy-done.10
  58.5 0.0 all-gather.10.cloned.1.call-update
  58.5 0.0 all-gather.8.cloned.1.call-start
  58.6 4.3 %collective-permute-start = (bf16[128,2048]{1,0:T(8,128)(2,1)}, bf16[128,2048]{1,0:T(8,128)(2,1)S(1)}, u32[]{:S(2)}, u32[]{:S(2)}) collective-permute-start(bf16[128,2048]{1,0:T(8,128)(2,1)} %copy-done.7), channel_id=1, source_target_pairs={{0,2},{2,4},{4,6},{6,8},{8,10},{10,12},{12,14},{14,16},{16,18},{18... | collective-permute-start | bytes 1572872 | tf_op jit(solution)/shard_map/ppermute | solution.py:19
  62.9 10.5 %collective-permute-done = bf16[128,2048]{1,0:T(8,128)(2,1)S(1)} collective-permute-done((bf16[128,2048]{1,0:T(8,128)(2,1)}, bf16[128,2048]{1,0:T(8,128)(2,1)S(1)}, u32[]{:S(2)}, u32[]{:S(2)}) %collective-permute-start) | collective-permute-done | bytes 524320 | tf_op jit(solution)/shard_map/ppermute | solution.py:19
  73.4 0.0 copy-start.11
  73.4 0.8 copy-done.11
  74.2 0.0 all-gather.8.cloned.1.call-update
  74.3 0.1 pad_add_fusion.place_ref
  74.3 0.0 all-gather.6.cloned.1.call-done.refs_0_.refs_1_
  74.3 0.0 all-gather.14.cloned.1.call-done.refs_8_.refs_9_
  74.3 0.0 all-gather.12.cloned.1.call-done.refs_6_.refs_7_
  74.4 0.0 all-gather.10.cloned.1.call-done.refs_4_.refs_5_
  74.4 8.6 %all-gather.8.cloned.1.call-done.refs_2_.refs_3_ = bf16[256,2048]{1,0:T(8,128)(2,1)} async-done(((bf16[128,2048]{1,0:T(8,128)(2,1)}), bf16[256,2048]{1,0:T(8,128)(2,1)}) %all-gather.8.cloned.1.call-update) | async-done | bytes 1048592 | tf_op jit(solution)/shard_map/all_gather | solution.py:121
  83.0 0.0 copy-done.6
  83.0 0.0 copy-done.5
  83.0 0.0 copy-start
  83.0 1.2 copy-done
  84.2 0.0 copy-start.1
  84.2 1.2 copy-done.1
  85.5 1.2 copy-done.2
  86.7 1.2 copy-done.3
  87.9 1.2 copy-done.4
  89.1 38.5 %attend.1 = bf16[128,8192]{1,0:T(8,128)(2,1)} custom-call(s32[2]{0:T(128)S(1)} %pad_add_fusion.place_ref, s32[12]{0:T(128)S(1)} %copy-done.6, bf16[128,8192]{1,0:T(8,128)(2,1)S(1)} %copy-done.5, bf16[256,2048]{1,0:T(8,128)(2,1)S(1)} %copy-done, bf16[256,2048]{1,0:T(8,128)(2,1)S(1)} %copy-done, bf16[256,2048]{1,0:T(8,128)(2,1)S(1)} %copy-done.4, ...), custom_call_target="tpu_custom_call" | custom-call | tf_op jit(solution)/shard_map/attend/pallas_call | solution.py:130
  (3 shorter events, 0.0 us)
Async XLA Ops:
  6.5 76.5 %copy-start.6 = (s32[12]{0:T(128)S(1)}, s32[12]{0:T(128)}, u32[]{:S(2)}) copy-start(s32[12]{0:T(128)} %lengths_ref.1) | copy-start | bytes 148
  6.5 76.5 %copy-start.5 = (bf16[128,8192]{1,0:T(8,128)(2,1)S(1)}, bf16[128,8192]{1,0:T(8,128)(2,1)}, u32[]{:S(2)}) copy-start(bf16[128,8192]{1,0:T(8,128)(2,1)} %q_ref.1) | copy-start | bytes 6291460
  6.5 67.8 %all-gather.6.cloned.1.call-start = ((), (), s32[]{:S(2)}) async-start(), calls=%async_computation | async-start | bytes 1572864 | tf_op jit(solution)/shard_map/all_gather | solution.py:121
  8.6 0.8 copy-start.7
  9.5 64.9 %all-gather.14.cloned.1.call-start = ((), (), s32[]{:S(2)}) async-start(), calls=%async_computation.4 | async-start | bytes 1572864 | tf_op jit(solution)/shard_map/all_gather | solution.py:121
  9.5 15.8 %collective-permute-start.3 = (bf16[128,2048]{1,0:T(8,128)(2,1)}, bf16[128,2048]{1,0:T(8,128)(2,1)S(1)}, u32[]{:S(2)}, u32[]{:S(2)}) collective-permute-start(bf16[128,2048]{1,0:T(8,128)(2,1)} %copy-done.7), channel_id=1, source_target_pairs={{0,8},{2,10},{4,12},{6,14},{8,16},{10,18},{12,20},{14,22},{16,24},... | collective-permute-start | bytes 1572872 | tf_op jit(solution)/shard_map/ppermute | solution.py:19
  25.3 0.8 copy-start.8
  26.1 48.3 %all-gather.12.cloned.1.call-start = ((), (), s32[]{:S(2)}) async-start(), calls=%async_computation.3 | async-start | bytes 1572864 | tf_op jit(solution)/shard_map/all_gather | solution.py:121
  26.1 15.8 %collective-permute-start.2 = (bf16[128,2048]{1,0:T(8,128)(2,1)}, bf16[128,2048]{1,0:T(8,128)(2,1)S(1)}, u32[]{:S(2)}, u32[]{:S(2)}) collective-permute-start(bf16[128,2048]{1,0:T(8,128)(2,1)} %copy-done.7), channel_id=1, source_target_pairs={{0,6},{2,8},{4,10},{6,12},{8,14},{10,16},{12,18},{14,20},{16,22},{... | collective-permute-start | bytes 1572872 | tf_op jit(solution)/shard_map/ppermute | solution.py:19
  41.9 0.8 copy-start.9
  42.8 31.6 %all-gather.10.cloned.1.call-start = ((), (), s32[]{:S(2)}) async-start(), calls=%async_computation.2 | async-start | bytes 1572864 | tf_op jit(solution)/shard_map/all_gather | solution.py:121
  42.8 14.9 %collective-permute-start.1 = (bf16[128,2048]{1,0:T(8,128)(2,1)}, bf16[128,2048]{1,0:T(8,128)(2,1)S(1)}, u32[]{:S(2)}, u32[]{:S(2)}) collective-permute-start(bf16[128,2048]{1,0:T(8,128)(2,1)} %copy-done.7), channel_id=1, source_target_pairs={{0,4},{2,6},{4,8},{6,10},{8,12},{10,14},{12,16},{14,18},{16,20},{1... | collective-permute-start | bytes 1572872 | tf_op jit(solution)/shard_map/ppermute | solution.py:19
  57.7 0.8 copy-start.10
  58.5 24.5 %all-gather.8.cloned.1.call-start = ((), (), s32[]{:S(2)}) async-start(), calls=%async_computation.1 | async-start | bytes 1572864 | tf_op jit(solution)/shard_map/all_gather | solution.py:121
  58.6 14.9 %collective-permute-start = (bf16[128,2048]{1,0:T(8,128)(2,1)}, bf16[128,2048]{1,0:T(8,128)(2,1)S(1)}, u32[]{:S(2)}, u32[]{:S(2)}) collective-permute-start(bf16[128,2048]{1,0:T(8,128)(2,1)} %copy-done.7), channel_id=1, source_target_pairs={{0,2},{2,4},{4,6},{6,8},{8,10},{10,12},{12,14},{14,16},{16,18},{18... | collective-permute-start | bytes 1572872 | tf_op jit(solution)/shard_map/ppermute | solution.py:19
  73.4 0.8 copy-start.11
  83.0 1.2 copy-start
  84.2 1.2 copy-start.1
  85.5 1.2 copy-start.2
  86.7 1.2 copy-start.3
  87.9 1.2 copy-start.4
Sparse Core Ops, SparseCore 0:
  9.6 10.4 all-gather.5
  26.2 10.4 all-gather.13
  42.9 10.4 all-gather.11
  58.7 10.3 all-gather.9
  74.4 8.5 all-gather.7

commit v2 on v1

v2 whole, which is shorter than its diff:
```python
import functools
import math

import jax
import jax.numpy as jnp
from jax import lax
from jax.experimental import pallas as pl
from jax.experimental.pallas import tpu as pltpu
from jax.sharding import PartitionSpec as P

HD = 128
REACH = 4
NEVER = -1e30
SUM_ROWS = 16


def from_behind(block, axis, distance):
    devices = range(lax.axis_size(axis))
    route = [(i - distance, i) for i in devices if i - distance in devices]
    return lax.ppermute(block, axis, route)


def swapped(block):
    return lax.ppermute(block, "head", [(0, 1), (1, 0)])


def attend_kernel(place_ref, lengths_ref, q_ref, *refs, group_size, chunk_heads):
    kv_refs, (out_ref, lo_ref, qt_ref, max_ref, acc_ref) = refs[:-5], refs[-5:]
    rows = q_ref.shape[0]
    span_rows = 2 * rows
    chunk = chunk_heads * rows
    first_query = place_ref[0]
    half = place_ref[1]
    own_start = first_query - half * rows
    last_query = first_query + rows - 1
    score_scale = HD ** (-0.5) * math.log2(math.e)

    @pl.when(pl.program_id(0) == 0)
    def _():
        pos = first_query + lax.broadcasted_iota(jnp.int32, (8, rows), 1)

        def later_doc(i, carry):
            start, lo = carry
            start = start + lengths_ref[i]
            return start, jnp.where(start <= pos, start, lo)

        _, lo = lax.fori_loop(
            0, lengths_ref.shape[0], later_doc, (jnp.int32(0), jnp.zeros((8, rows), jnp.int32))
        )
        lo_ref[...] = lo

    def doc_start(i, carry):
        start, lo_first, lo_last = carry
        start = start + lengths_ref[i]
        lo_first = jnp.where(start <= first_query, start, lo_first)
        lo_last = jnp.where(start <= last_query, start, lo_last)
        return start, lo_first, lo_last

    zero = jnp.int32(0)
    _, lo_first, lo_last = lax.fori_loop(0, lengths_ref.shape[0], doc_start, (zero, zero, zero))

    for h in range(group_size):
        qt_ref[:, h * rows : (h + 1) * rows] = q_ref[:, h * HD : (h + 1) * HD].T

    def absorb(key_block, value_block, allowed, initial):
        keys = key_block.shape[0]
        widened = jnp.concatenate([value_block.T, jnp.ones((SUM_ROWS, keys), value_block.dtype)], axis=0)
        if allowed is not None:
            allowed = jnp.concatenate([allowed] * chunk_heads, axis=1)
        for i in range(group_size // chunk_heads):
            at = slice(i * chunk, (i + 1) * chunk)
            scores = jnp.dot(key_block, qt_ref[:, at], preferred_element_type=jnp.float32)
            if allowed is not None:
                scores = jnp.where(allowed, scores, NEVER)
            max_new = jnp.max(scores, axis=0, keepdims=True)
            if not initial:
                max_old = max_ref[:, at]
                max_new = jnp.maximum(max_old, max_new)
            weights = jnp.exp2((scores - max_new) * score_scale).astype(jnp.bfloat16)
            added = jnp.dot(widened, weights, preferred_element_type=jnp.float32)
            if not initial:
                added = acc_ref[:, at] * jnp.exp2((max_old - max_new) * score_scale) + added
            acc_ref[:, at] = added
            max_ref[:, at] = max_new

    def positions(start, keys):
        return start + lax.broadcasted_iota(jnp.int32, (keys, rows), 0)

    def lows(keys):
        return jnp.concatenate([lo_ref[...]] * (keys // 8), axis=0)

    query_pos = first_query + lax.broadcasted_iota(jnp.int32, (rows, rows), 1)
    key_pos = positions(first_query, rows)
    absorb(kv_refs[0][...], kv_refs[1][...], (key_pos >= lows(rows)) & (key_pos <= query_pos), True)

    @pl.when((half == 1) & (own_start + rows > lo_first))
    def _():
        absorb(kv_refs[2][...], kv_refs[3][...], positions(own_start, rows) >= lows(rows), False)

    for distance in range(1, len(kv_refs) // 4):
        start = own_start - distance * span_rows
        k_near, v_near, k_far, v_far = kv_refs[4 * distance : 4 * distance + 4]

        def span(masked, k_near=k_near, v_near=v_near, k_far=k_far, v_far=v_far, start=start):
            allowed = None
            if masked:
                allowed = (
                    jnp.concatenate(
                        [positions(start + half * rows, rows), positions(start + (1 - half) * rows, rows)], axis=0
                    )
                    >= lows(span_rows)
                )
            absorb(
                jnp.concatenate([k_near[...], k_far[...]], axis=0),
                jnp.concatenate([v_near[...], v_far[...]], axis=0),
                allowed,
                False,
            )

        @pl.when((start + span_rows > lo_first) & (start < lo_last))
        def _():
            span(True)

        @pl.when(start >= lo_last)
        def _():
            span(False)

    for h in range(group_size):
        at = slice(h * rows, (h + 1) * rows)
        finished = acc_ref[:HD, at] * (1.0 / acc_ref[HD : HD + 1, at])
        out_ref[:, h * HD : (h + 1) * HD] = finished.astype(jnp.bfloat16).T


def per_device(queries, keys, values, doc_lengths):
    rows = queries.shape[0]
    kv_heads = keys.shape[1] // HD
    group_size = queries.shape[1] // keys.shape[1]
    half = lax.axis_index("head")
    span = lax.axis_index("ctx")
    place = jnp.stack([(span * lax.axis_size("head") + half) * rows, half]).astype(jnp.int32)

    own = jnp.concatenate([keys, values], axis=1)
    near = [own] + [from_behind(own, "ctx", d) for d in range(REACH, 0, -1)][::-1]
    far = [swapped(block) for block in near]

    smem = pl.BlockSpec(memory_space=pltpu.SMEM)
    kv_specs, kv_args = [], []
    for pair in zip(near, far):
        for block in pair:
            kv_specs.append(pl.BlockSpec((rows, HD), lambda g: (0, g)))
            kv_specs.append(pl.BlockSpec((rows, HD), lambda g: (0, kv_heads + g)))
            kv_args += [block, block]
    head_rows = group_size * rows
    return pl.pallas_call(
        functools.partial(attend_kernel, group_size=group_size, chunk_heads=2),
        grid=(kv_heads,),
        in_specs=[smem, smem, pl.BlockSpec((rows, group_size * HD), lambda g: (0, g))] + kv_specs,
        out_specs=pl.BlockSpec((rows, group_size * HD), lambda g: (0, g)),
        out_shape=jax.ShapeDtypeStruct(queries.shape, queries.dtype),
        scratch_shapes=[
            pltpu.VMEM((8, rows), jnp.int32),
            pltpu.VMEM((HD, head_rows), jnp.bfloat16),
            pltpu.VMEM((1, head_rows), jnp.float32),
            pltpu.VMEM((HD + SUM_ROWS, head_rows), jnp.float32),
        ],
        compiler_params=pltpu.CompilerParams(
            dimension_semantics=("arbitrary",), vmem_limit_bytes=32 * 1024 * 1024
        ),
        name="attend",
    )(place, doc_lengths, queries, *kv_args)


def solution(mesh):
    placed = P(("ctx", "head"), None)
    return jax.shard_map(
        per_device, mesh=mesh, in_specs=(placed, placed, placed, P()), out_specs=placed, check_vma=False
    )
```

time: 136 us -> 107 us (0.79); the launches traced: 134 us -> 107 us
  waiting for transfers between devices: 54.4 us -> 39.2 us
  between operations: 13.2 us -> 0.07 us
  Pallas kernels: 38.5 us -> 49.7 us
  local copies, waits for them, and re-layouts: 12.2 us -> 4.18 us
  starting transfers between devices: 15.7 us -> 13.9 us
    pallas_call x1, Pallas kernels: 38.5 us -> 49.7 us  [per_device(): pl.pallas_call(functools.partial(attend_kernel, group_size=group_size, ch...]
    all_gather x5 -> x0, waiting for transfers between devices: 8.65 us -> none  [per_device(): lax.all_gather(block, 'head', axis=0, tiled=True)]
    ppermute x4, waiting for transfers between devices: 45.7 us -> 37.3 us  [from_behind(): return lax.ppermute(block, axis, route)]
    unnamed x25 -> x5, local copies, waits for them, and re-layouts: 11.2 us -> 3.21 us
    ppermute x0 -> x5, waiting for transfers between devices: none -> 1.95 us  [swapped(): return lax.ppermute(block, 'head', [(0, 1), (1, 0)])]
    ppermute x4, starting transfers between devices: 15.6 us -> 13.8 us  [from_behind(): return lax.ppermute(block, axis, route)]
where the time goes in v2:
time: 107 us
  Pallas kernels  49.7 us (46%)
  waiting for transfers between devices  39.2 us (37%)
  starting transfers between devices  13.9 us (13%)
  local copies, waits for them, and re-layouts  4.18 us (4%)
    pallas_call x1, Pallas kernels, per_device(): pl.pallas_call(functools.partial(attend_kernel, group_size=group_size, ch...  49.7 us
    ppermute x4, waiting for transfers between devices, from_behind(): return lax.ppermute(block, axis, route)  37.3 us
    ppermute x4, starting transfers between devices, from_behind(): return lax.ppermute(block, axis, route)  13.8 us
    unnamed x5, local copies, waits for them, and re-layouts  3.21 us
  transfers between devices with their start and end apart: 9, of which 5 were waited for; matrix products, arithmetic and copies ran while one was open for 0% of the time, Pallas kernels for 0%

profile of v2, /device:TPU:8, one launch (start us, length us, event | category | flops | bytes accessed | tf_op | source)
XLA Modules:
  0.0 107.1 jit_solution(12135990775792168947)
XLA Ops:
  0.0 1.0 constant_dynamic-update-slice_fusion.1
  1.0 1.0 constant_dynamic-update-slice_fusion.refs_0_.refs_1_
  1.9 3.5 %collective-permute-start.7 = (bf16[128,2048]{1,0:T(8,128)(2,1)S(1)}, bf16[128,2048]{1,0:T(8,128)(2,1)S(1)}, u32[]{:S(2)}, u32[]{:S(2)}) collective-permute-start(bf16[128,2048]{1,0:T(8,128)(2,1)S(1)} %constant_dynamic-update-slice_fusion.refs_0_.refs_1_), channel_id=1, source_target_pairs={{0,8},{2,10},{4,12},{6,14},{8,16},{10,18},{12,20},{14,22},{16,24},... | collective-permute-start | bytes 1572872 | tf_op jit(solution)/shard_map/ppermute | solution.py:20
  5.4 4.4 %collective-permute-start.5 = (bf16[128,2048]{1,0:T(8,128)(2,1)S(1)}, bf16[128,2048]{1,0:T(8,128)(2,1)S(1)}, u32[]{:S(2)}, u32[]{:S(2)}) collective-permute-start(bf16[128,2048]{1,0:T(8,128)(2,1)S(1)} %constant_dynamic-update-slice_fusion.refs_0_.refs_1_), channel_id=1, source_target_pairs={{0,6},{2,8},{4,10},{6,12},{8,14},{10,16},{12,18},{14,20},{16,22},{... | collective-permute-start | bytes 1572872 | tf_op jit(solution)/shard_map/ppermute | solution.py:20
  9.8 3.4 %collective-permute-start.3 = (bf16[128,2048]{1,0:T(8,128)(2,1)S(1)}, bf16[128,2048]{1,0:T(8,128)(2,1)S(1)}, u32[]{:S(2)}, u32[]{:S(2)}) collective-permute-start(bf16[128,2048]{1,0:T(8,128)(2,1)S(1)} %constant_dynamic-update-slice_fusion.refs_0_.refs_1_), channel_id=1, source_target_pairs={{0,4},{2,6},{4,8},{6,10},{8,12},{10,14},{12,16},{14,18},{16,20},{1... | collective-permute-start | bytes 1572872 | tf_op jit(solution)/shard_map/ppermute | solution.py:20
  13.2 2.5 %collective-permute-start.1 = (bf16[128,2048]{1,0:T(8,128)(2,1)S(1)}, bf16[128,2048]{1,0:T(8,128)(2,1)S(1)}, u32[]{:S(2)}, u32[]{:S(2)}) collective-permute-start(bf16[128,2048]{1,0:T(8,128)(2,1)S(1)} %constant_dynamic-update-slice_fusion.refs_0_.refs_1_), channel_id=1, source_target_pairs={{0,2},{2,4},{4,6},{6,8},{8,10},{10,12},{12,14},{14,16},{16,18},{18... | collective-permute-start | bytes 1572872 | tf_op jit(solution)/shard_map/ppermute | solution.py:20
  15.7 0.1 collective-permute-start
  15.8 1.7 %collective-permute-done.7.refs_16_.refs_17_ = bf16[128,2048]{1,0:T(8,128)(2,1)S(1)} collective-permute-done((bf16[128,2048]{1,0:T(8,128)(2,1)S(1)}, bf16[128,2048]{1,0:T(8,128)(2,1)S(1)}, u32[]{:S(2)}, u32[]{:S(2)}) %collective-permute-start.7) | collective-permute-done | bytes 524320 | tf_op jit(solution)/shard_map/ppermute | solution.py:20
  17.5 0.0 collective-permute-start.8
  17.5 12.3 %collective-permute-done.5.refs_12_.refs_13_ = bf16[128,2048]{1,0:T(8,128)(2,1)S(1)} collective-permute-done((bf16[128,2048]{1,0:T(8,128)(2,1)S(1)}, bf16[128,2048]{1,0:T(8,128)(2,1)S(1)}, u32[]{:S(2)}, u32[]{:S(2)}) %collective-permute-start.5) | collective-permute-done | bytes 524320 | tf_op jit(solution)/shard_map/ppermute | solution.py:20
  29.8 0.0 collective-permute-start.6
  29.8 11.3 %collective-permute-done.3.refs_8_.refs_9_ = bf16[128,2048]{1,0:T(8,128)(2,1)S(1)} collective-permute-done((bf16[128,2048]{1,0:T(8,128)(2,1)S(1)}, bf16[128,2048]{1,0:T(8,128)(2,1)S(1)}, u32[]{:S(2)}, u32[]{:S(2)}) %collective-permute-start.3) | collective-permute-done | bytes 524320 | tf_op jit(solution)/shard_map/ppermute | solution.py:20
  41.1 0.0 collective-permute-start.4
  41.1 12.0 %collective-permute-done.1.refs_4_.refs_5_ = bf16[128,2048]{1,0:T(8,128)(2,1)S(1)} collective-permute-done((bf16[128,2048]{1,0:T(8,128)(2,1)S(1)}, bf16[128,2048]{1,0:T(8,128)(2,1)S(1)}, u32[]{:S(2)}, u32[]{:S(2)}) %collective-permute-start.1) | collective-permute-done | bytes 524320 | tf_op jit(solution)/shard_map/ppermute | solution.py:20
  53.1 0.0 collective-permute-start.2
  53.1 0.1 pad_add_fusion.place_ref
  53.2 0.0 collective-permute-done.refs_2_.refs_3_
  53.2 0.0 collective-permute-done.8.refs_18_.refs_19_
  53.2 0.0 collective-permute-done.6.refs_14_.refs_15_
  53.2 0.0 collective-permute-done.4.refs_10_.refs_11_
  53.2 1.9 %collective-permute-done.2.refs_6_.refs_7_ = bf16[128,2048]{1,0:T(8,128)(2,1)} collective-permute-done((bf16[128,2048]{1,0:T(8,128)(2,1)S(1)}, bf16[128,2048]{1,0:T(8,128)(2,1)}, u32[]{:S(2)}, u32[]{:S(2)}) %collective-permute-start.2) | collective-permute-done | bytes 524320 | tf_op jit(solution)/shard_map/ppermute | solution.py:24
  55.2 0.0 copy-start
  55.2 1.6 %copy-done = bf16[128,8192]{1,0:T(8,128)(2,1)S(1)} copy-done((bf16[128,8192]{1,0:T(8,128)(2,1)S(1)}, bf16[128,8192]{1,0:T(8,128)(2,1)}, u32[]{:S(2)}) %copy-start) | copy-done | bytes 2097176
  56.7 0.0 copy-start.1
  56.7 0.7 copy-done.1
  57.4 49.7 %attend.1 = bf16[128,8192]{1,0:T(8,128)(2,1)} custom-call(s32[2]{0:T(128)S(1)} %pad_add_fusion.place_ref, s32[12]{0:T(128)S(1)} %copy-done.1, bf16[128,8192]{1,0:T(8,128)(2,1)S(1)} %copy-done, bf16[128,2048]{1,0:T(8,128)(2,1)S(1)} %constant_dynamic-update-slice_fusion.refs_0_.refs_1_, ...), custom_call_target="tpu_custom_call" | custom-call | tf_op jit(solution)/shard_map/attend/pallas_call | solution.py:154
Async XLA Ops:
  1.9 15.6 %collective-permute-start.7 = (bf16[128,2048]{1,0:T(8,128)(2,1)S(1)}, bf16[128,2048]{1,0:T(8,128)(2,1)S(1)}, u32[]{:S(2)}, u32[]{:S(2)}) collective-permute-start(bf16[128,2048]{1,0:T(8,128)(2,1)S(1)} %constant_dynamic-update-slice_fusion.refs_0_.refs_1_), channel_id=1, source_target_pairs={{0,8},{2,10},{4,12},{6,14},{8,16},{10,18},{12,20},{14,22},{16,24},... | collective-permute-start | bytes 1572872 | tf_op jit(solution)/shard_map/ppermute | solution.py:20
  5.4 24.3 %collective-permute-start.5 = (bf16[128,2048]{1,0:T(8,128)(2,1)S(1)}, bf16[128,2048]{1,0:T(8,128)(2,1)S(1)}, u32[]{:S(2)}, u32[]{:S(2)}) collective-permute-start(bf16[128,2048]{1,0:T(8,128)(2,1)S(1)} %constant_dynamic-update-slice_fusion.refs_0_.refs_1_), channel_id=1, source_target_pairs={{0,6},{2,8},{4,10},{6,12},{8,14},{10,16},{12,18},{14,20},{16,22},{... | collective-permute-start | bytes 1572872 | tf_op jit(solution)/shard_map/ppermute | solution.py:20
  9.8 31.3 %collective-permute-start.3 = (bf16[128,2048]{1,0:T(8,128)(2,1)S(1)}, bf16[128,2048]{1,0:T(8,128)(2,1)S(1)}, u32[]{:S(2)}, u32[]{:S(2)}) collective-permute-start(bf16[128,2048]{1,0:T(8,128)(2,1)S(1)} %constant_dynamic-update-slice_fusion.refs_0_.refs_1_), channel_id=1, source_target_pairs={{0,4},{2,6},{4,8},{6,10},{8,12},{10,14},{12,16},{14,18},{16,20},{1... | collective-permute-start | bytes 1572872 | tf_op jit(solution)/shard_map/ppermute | solution.py:20
  13.2 39.9 %collective-permute-start.1 = (bf16[128,2048]{1,0:T(8,128)(2,1)S(1)}, bf16[128,2048]{1,0:T(8,128)(2,1)S(1)}, u32[]{:S(2)}, u32[]{:S(2)}) collective-permute-start(bf16[128,2048]{1,0:T(8,128)(2,1)S(1)} %constant_dynamic-update-slice_fusion.refs_0_.refs_1_), channel_id=1, source_target_pairs={{0,2},{2,4},{4,6},{6,8},{8,10},{10,12},{12,14},{14,16},{16,18},{18... | collective-permute-start | bytes 1572872 | tf_op jit(solution)/shard_map/ppermute | solution.py:20
  15.7 37.4 %collective-permute-start = (bf16[128,2048]{1,0:T(8,128)(2,1)S(1)}, bf16[128,2048]{1,0:T(8,128)(2,1)S(1)}, u32[]{:S(2)}, u32[]{:S(2)}) collective-permute-start(bf16[128,2048]{1,0:T(8,128)(2,1)S(1)} %constant_dynamic-update-slice_fusion.refs_0_.refs_1_), channel_id=1, source_target_pairs={{0,1},{1,0},{2,3},{3,2},{4,5},{5,4},{6,7},{7,6},{8,9},{9,8},{10,11... | collective-permute-start | bytes 1572872 | tf_op jit(solution)/shard_map/ppermute | solution.py:24
  17.5 35.7 %collective-permute-start.8 = (bf16[128,2048]{1,0:T(8,128)(2,1)S(1)}, bf16[128,2048]{1,0:T(8,128)(2,1)}, u32[]{:S(2)}, u32[]{:S(2)}) collective-permute-start(bf16[128,2048]{1,0:T(8,128)(2,1)S(1)} %collective-permute-done.7.refs_16_.refs_17_), channel_id=1, source_target_pairs={{0,1},{1,0},{2,3},{3,2},{4,5},{5,4},{6,7},{7,6},{8,9},{9,8},{10,11... | collective-permute-start | bytes 1572872 | tf_op jit(solution)/shard_map/ppermute | solution.py:24
  29.8 23.4 %collective-permute-start.6 = (bf16[128,2048]{1,0:T(8,128)(2,1)S(1)}, bf16[128,2048]{1,0:T(8,128)(2,1)}, u32[]{:S(2)}, u32[]{:S(2)}) collective-permute-start(bf16[128,2048]{1,0:T(8,128)(2,1)S(1)} %collective-permute-done.5.refs_12_.refs_13_), channel_id=1, source_target_pairs={{0,1},{1,0},{2,3},{3,2},{4,5},{5,4},{6,7},{7,6},{8,9},{9,8},{10,11... | collective-permute-start | bytes 1572872 | tf_op jit(solution)/shard_map/ppermute | solution.py:24
  41.1 12.1 %collective-permute-start.4 = (bf16[128,2048]{1,0:T(8,128)(2,1)S(1)}, bf16[128,2048]{1,0:T(8,128)(2,1)}, u32[]{:S(2)}, u32[]{:S(2)}) collective-permute-start(bf16[128,2048]{1,0:T(8,128)(2,1)S(1)} %collective-permute-done.3.refs_8_.refs_9_), channel_id=1, source_target_pairs={{0,1},{1,0},{2,3},{3,2},{4,5},{5,4},{6,7},{7,6},{8,9},{9,8},{10,11... | collective-permute-start | bytes 1572872 | tf_op jit(solution)/shard_map/ppermute | solution.py:24
  53.1 2.0 %collective-permute-start.2 = (bf16[128,2048]{1,0:T(8,128)(2,1)S(1)}, bf16[128,2048]{1,0:T(8,128)(2,1)}, u32[]{:S(2)}, u32[]{:S(2)}) collective-permute-start(bf16[128,2048]{1,0:T(8,128)(2,1)S(1)} %collective-permute-done.1.refs_4_.refs_5_), channel_id=1, source_target_pairs={{0,1},{1,0},{2,3},{3,2},{4,5},{5,4},{6,7},{7,6},{8,9},{9,8},{10,11... | collective-permute-start | bytes 1572872 | tf_op jit(solution)/shard_map/ppermute | solution.py:24
  55.2 1.6 %copy-start = (bf16[128,8192]{1,0:T(8,128)(2,1)S(1)}, bf16[128,8192]{1,0:T(8,128)(2,1)}, u32[]{:S(2)}) copy-start(bf16[128,8192]{1,0:T(8,128)(2,1)} %q_ref.1) | copy-start | bytes 6291460
  56.7 0.7 copy-start.1

commit v3 on v0

v3 whole, which is shorter than its diff:
```python
import functools
import math

import jax
import jax.numpy as jnp
from jax import lax
from jax.experimental import pallas as pl
from jax.experimental.pallas import tpu as pltpu
from jax.sharding import PartitionSpec as P

HD = 128
REACH = 4
NEVER = -1e30
SUM_ROWS = 16
AXES = ("ctx", "head")
PARTNER = ((1, 2, 3), (2, 1, 3))


def to_next_group(block):
    spans, cores = lax.axis_size("ctx"), lax.axis_size("head")
    pairs = [(s * cores + h, (s + REACH) * cores + h) for s in range(spans - REACH) for h in range(cores)]
    return lax.ppermute(block, AXES, pairs)


def in_group(block, turn):
    spans, cores = lax.axis_size("ctx"), lax.axis_size("head")
    pairs = []
    for s in range(spans):
        for h in range(cores):
            pairs.append((s * cores + h, (s ^ PARTNER[h][turn]) * cores + h))
    return lax.ppermute(block, AXES, pairs)


def to_other_core(block):
    cores = lax.axis_size("head")
    return lax.ppermute(block, "head", [(h, cores - 1 - h) for h in range(cores)])


def doc_starts(lengths_ref, first, last):
    def one_doc(i, carry):
        start, lo_first, lo_last = carry
        start = start + lengths_ref[i]
        return start, jnp.where(start <= first, start, lo_first), jnp.where(start <= last, start, lo_last)

    zero = jnp.int32(0)
    _, lo_first, lo_last = lax.fori_loop(0, lengths_ref.shape[0], one_doc, (zero, zero, zero))
    return lo_first, lo_last


def doc_start_rows(lengths_ref, first_query, rows):
    pos = first_query + lax.broadcasted_iota(jnp.int32, (8, rows), 1)

    def one_doc(i, carry):
        start, lo = carry
        start = start + lengths_ref[i]
        return start, jnp.where(start <= pos, start, lo)

    zero = jnp.zeros((8, rows), jnp.int32)
    return lax.fori_loop(0, lengths_ref.shape[0], one_doc, (jnp.int32(0), zero))[1]


def head_group(g, width):
    return pl.ds(pl.multiple_of(g * width, width), width)


def absorb(key_block, value_block, allowed, state, at, initial, group_size):
    qt_ref, max_ref, acc_ref = state
    keys = key_block.shape[0]
    widened = jnp.concatenate([value_block.T, jnp.ones((SUM_ROWS, keys), value_block.dtype)], axis=0)
    scores = jnp.dot(key_block, qt_ref[:, at], preferred_element_type=jnp.float32)
    if allowed is not None:
        scores = jnp.where(jnp.concatenate([allowed] * group_size, axis=1), scores, NEVER)
    max_new = jnp.max(scores, axis=0, keepdims=True)
    score_scale = HD ** (-0.5) * math.log2(math.e)
    if not initial:
        max_old = max_ref[:1, at]
        max_new = jnp.maximum(max_old, max_new)
    weights = jnp.exp2((scores - max_new) * score_scale).astype(jnp.bfloat16)
    added = jnp.dot(widened, weights, preferred_element_type=jnp.float32)
    if not initial:
        added = acc_ref[:, at] * jnp.exp2((max_old - max_new) * score_scale) + added
    acc_ref[:, at] = added
    max_ref[:, at] = jnp.broadcast_to(max_new, (8, max_new.shape[1]))


def positions(start, keys, queries):
    return start + lax.broadcasted_iota(jnp.int32, (keys, queries), 0)


def own_kernel(place_ref, lengths_ref, q_ref, near_ref, far_ref, qt_ref, max_ref, acc_ref, *, group_size):
    rows = q_ref.shape[0]
    width = group_size * rows
    first_query, half = place_ref[0], place_ref[1]
    own_start = first_query - half * rows
    lo_first, _ = doc_starts(lengths_ref, first_query, first_query)
    lo = doc_start_rows(lengths_ref, first_query, rows)
    lo = jnp.concatenate([lo] * (rows // 8), axis=0)
    query_pos = first_query + lax.broadcasted_iota(jnp.int32, (rows, rows), 1)
    key_pos = positions(first_query, rows, rows)
    own_allowed = (key_pos >= lo) & (key_pos <= query_pos)
    far_allowed = positions(own_start, rows, rows) >= lo
    state = (qt_ref, max_ref, acc_ref)

    def one_group(g, _):
        at = head_group(g, width)
        kv = head_group(g, HD)
        q = q_ref[:, head_group(g, group_size * HD)]
        qt_ref[:, at] = jnp.concatenate([q[:, h * HD : (h + 1) * HD].T for h in range(group_size)], axis=1)
        absorb(near_ref[0, :, kv], near_ref[1, :, kv], own_allowed, state, at, True, group_size)

        @pl.when((half == 1) & (own_start + rows > lo_first))
        def _():
            absorb(far_ref[0, :, kv], far_ref[1, :, kv], far_allowed, state, at, False, group_size)

        return 0

    lax.fori_loop(0, near_ref.shape[2] // HD, one_group, 0)


def span_kernel(place_ref, lengths_ref, near_ref, far_ref, qt_ref, max_in, acc_in, *refs, group_size, last):
    del max_in, acc_in
    out_ref = refs[0] if last else None
    max_ref, acc_ref = refs[-2:]
    rows = near_ref.shape[1]
    width = group_size * rows
    kv_heads = near_ref.shape[2] // HD
    first_query, half, near_start, far_start = place_ref[0], place_ref[1], place_ref[2], place_ref[3]
    lo_first, lo_last = doc_starts(lengths_ref, first_query, first_query + rows - 1)
    state = (qt_ref, max_ref, acc_ref)

    def span(masked):
        allowed = None
        if masked:
            lo = jnp.concatenate([doc_start_rows(lengths_ref, first_query, rows)] * (rows // 4), axis=0)
            key_pos = jnp.concatenate([positions(near_start, rows, rows), positions(far_start, rows, rows)], axis=0)
            allowed = key_pos >= lo

        def one_group(g, _):
            kv = head_group(g, HD)
            absorb(
                jnp.concatenate([near_ref[0, :, kv], far_ref[0, :, kv]], axis=0),
                jnp.concatenate([near_ref[1, :, kv], far_ref[1, :, kv]], axis=0),
                allowed,
                state,
                head_group(g, width),
                False,
                group_size,
            )
            return 0

        lax.fori_loop(0, kv_heads, one_group, 0)

    needed = jnp.maximum(near_start, far_start) + rows > lo_first
    whole = jnp.minimum(near_start, far_start) >= lo_last

    @pl.when(needed & jnp.logical_not(whole))
    def _():
        span(True)

    @pl.when(whole)
    def _():
        span(False)

    if last:

        def finish(g, _):
            acc = acc_ref[:, head_group(g, width)]
            finished = (acc[:HD] * (1.0 / acc[HD : HD + 1])).astype(jnp.bfloat16)
            out_ref[:, head_group(g, group_size * HD)] = jnp.concatenate(
                [finished[:, h * rows : (h + 1) * rows].T for h in range(group_size)], axis=1
            )
            return 0

        lax.fori_loop(0, kv_heads, finish, 0)


def per_device(queries, keys, values, doc_lengths):
    rows = queries.shape[0]
    group_size = queries.shape[1] // keys.shape[1]
    head_rows = (queries.shape[1] // HD) * rows
    half, span = lax.axis_index("head"), lax.axis_index("ctx")
    cores = lax.axis_size("head")
    place_in_group = lax.rem(span, REACH)
    first_query = (span * cores + half) * rows

    vmem = pl.BlockSpec(memory_space=pltpu.VMEM)
    smem = pl.BlockSpec(memory_space=pltpu.SMEM)
    qt_shape = jax.ShapeDtypeStruct((HD, head_rows), queries.dtype)
    max_shape = jax.ShapeDtypeStruct((8, head_rows), jnp.float32)
    acc_shape = jax.ShapeDtypeStruct((HD + SUM_ROWS, head_rows), jnp.float32)
    params = pltpu.CompilerParams(vmem_limit_bytes=24 * 1024 * 1024)

    cost = pl.CostEstimate(flops=0, bytes_accessed=0, transcendentals=0)

    own = jnp.stack([keys, values])
    behind = to_next_group(own)
    own_far = to_other_core(own)

    def place(near_span, far_span):
        near_start = (near_span * cores + half) * rows
        far_start = (far_span * cores + 1 - half) * rows
        return jnp.stack([first_query, half, near_start, far_start]).astype(jnp.int32)

    qt, row_max, acc = pl.pallas_call(
        functools.partial(own_kernel, group_size=group_size),
        in_specs=[smem, smem, vmem, vmem, vmem],
        out_specs=(vmem, vmem, vmem),
        out_shape=(qt_shape, max_shape, acc_shape),
        compiler_params=params,
        cost_estimate=cost,
        name="attend_own",
    )(place(span, span), doc_lengths, queries, own, own_far)

    behind, acc = lax.optimization_barrier((behind, acc))
    arrivals = [(span - REACH, span - REACH, behind)]
    for turn in range(REACH - 1):
        mine = jnp.where(half == 0, PARTNER[0][turn], PARTNER[1][turn])
        other = jnp.where(half == 0, PARTNER[1][turn], PARTNER[0][turn])
        send = jnp.where((place_in_group ^ mine) > place_in_group, own, behind)

        def source(partner):
            from_place = place_in_group ^ partner
            return span - place_in_group + from_place - jnp.where(from_place > place_in_group, REACH, 0)

        arrivals.append((source(mine), source(other), in_group(send, turn)))

    for number, (near_span, far_span, near) in enumerate(arrivals):
        last = number == len(arrivals) - 1
        if number > 0:
            near, acc = lax.optimization_barrier((near, acc))
        out_shapes = (max_shape, acc_shape)
        if last:
            out_shapes = (jax.ShapeDtypeStruct(queries.shape, queries.dtype),) + out_shapes
        *out, row_max, acc = pl.pallas_call(
            functools.partial(span_kernel, group_size=group_size, last=last),
            in_specs=[smem, smem] + [vmem] * 5,
            out_specs=(vmem,) * len(out_shapes),
            out_shape=out_shapes,
            input_output_aliases={5: len(out_shapes) - 2, 6: len(out_shapes) - 1},
            compiler_params=params,
            cost_estimate=cost,
            name="attend_last" if last else "attend_span",
        )(place(near_span, far_span), doc_lengths, near, to_other_core(near), qt, row_max, acc)
    return out[0]


def solution(mesh):
    placed = P(AXES, None)
    return jax.shard_map(
        per_device, mesh=mesh, in_specs=(placed, placed, placed, P()), out_specs=placed, check_vma=False
    )
```

time: 124 us -> 63 us (0.51)
  matrix products: 43.7 us -> 0 us
  Pallas kernels: 0 us -> 30.9 us
  local copies, waits for them, and re-layouts: 27.1 us -> 2.25 us
  waiting for transfers between devices: 1.42 us -> 17.7 us
  starting transfers between devices: 25.3 us -> 9.09 us
  other arithmetic: 14.7 us -> 2.37 us
  blocking collectives: 6.61 us -> 0 us
  between operations: 3.33 us -> 0.12 us
    dot_general x10 -> x0, matrix products: 43.7 us -> none  [the longest x5 31.9 us: update_tile(): jnp.einsum('qkgs,skd->qkgd', weights.astype(jnp.bfloat16), value_rows, pr...]
    pallas_call x0 -> x5, Pallas kernels: none -> 30.9 us  [the longest x4 26.1 us: per_device(): pl.pallas_call(functools.partial(span_kernel, group_size=group_size, last...]
    ppermute x4 -> x9, waiting for transfers between devices: 0.01 us -> 17.7 us  [the longest x3 9.95 us: in_group(): return lax.ppermute(block, AXES, pairs)]
    all_to_all x6 -> x0, local copies, waits for them, and re-layouts: 15.3 us -> none  [the longest x3 8.82 us: per_device(): lax.all_to_all(finished, 'head', split_axis=0, concat_axis=1, tiled=True)]
    all_to_all x3 -> x0, starting transfers between devices: 10.7 us -> none  [the longest x1 3.76 us: per_device(): lax.all_to_all(queries, 'head', split_axis=1, concat_axis=0, tiled=True)]
    reduce_sum x6 -> x0, other arithmetic: 9.17 us -> none  [the longest x5 9.07 us: update_tile(): sum_new = row_sum * rescale + jnp.sum(weights, axis=-1)]
    all_to_all x1 -> x0, blocking collectives: 6.61 us -> none  [per_device(): lax.all_to_all(finished, 'head', split_axis=0, concat_axis=1, tiled=True)]
    ppermute x4 -> x9, starting transfers between devices: 14.7 us -> 9.09 us  [the longest x3 5.52 us: in_group(): return lax.ppermute(block, AXES, pairs)]
  transfers between devices with their start and end apart: 7 -> 9, of which waited for: 1 -> 6; matrix products, arithmetic and copies ran while one was open for 46% -> 2% of each run, Pallas kernels for 0% -> 36%
where the time goes in v3:
time: 63 us; the launch traced here: 62.4 us
  Pallas kernels  30.9 us (49%)
  waiting for transfers between devices  17.7 us (28%)
  starting transfers between devices  9.09 us (14%)
  other arithmetic  2.37 us (4%)
  local copies, waits for them, and re-layouts  2.25 us (4%)
    pallas_call x4, Pallas kernels, per_device(): pl.pallas_call(functools.partial(span_kernel, group_size=group_size, last...  26.1 us
    ppermute x3, waiting for transfers between devices, in_group(): return lax.ppermute(block, AXES, pairs)  9.95 us
    ppermute x3, starting transfers between devices, in_group(): return lax.ppermute(block, AXES, pairs)  5.52 us
    ppermute x1, waiting for transfers between devices, to_next_group(): return lax.ppermute(block, AXES, pairs)  5.48 us
    pallas_call x1, Pallas kernels, per_device(): pl.pallas_call(functools.partial(own_kernel, group_size=group_size), in_s...  4.77 us
    ppermute x1, starting transfers between devices, to_next_group(): return lax.ppermute(block, AXES, pairs)  3.48 us
    ppermute x5, waiting for transfers between devices, to_other_core(): lax.ppermute(block, 'head', [(h, cores - 1 - h) for h in range(cores)])  2.3 us
    unnamed x4, local copies, waits for them, and re-layouts  2.25 us
  transfers between devices with their start and end apart: 9, of which 6 were waited for; matrix products, arithmetic and copies ran while one was open for 2% of the time, Pallas kernels for 36%

profile of v3, /device:TPU:8, one launch (start us, length us, event | category | flops | bytes accessed | tf_op | source)
XLA Modules:
  0.0 62.4 jit_solution(5105720375342297214)
XLA Ops:
  0.0 1.1 %pad_maximum_fusion.near_ref = bf16[2,128,1024]{2,1,0:T(8,128)(2,1)S(1)} fusion(bf16[1,128,1024]{2,1,0:T(8,128)(2,1)} %bitcast.13, bf16[1,128,1024]{2,1,0:T(8,128)(2,1)} %bitcast.15), kind=kLoop, calls=%fused_computation | loop fusion | flops 262144 | bytes 1048576 | tf_op jit(solution)/shard_map/stack | solution.py:195
  1.1 0.1 collective-permute-start.1
  1.2 3.5 %collective-permute-start = (bf16[2,128,1024]{2,1,0:T(8,128)(2,1)S(1)}, bf16[2,128,1024]{2,1,0:T(8,128)(2,1)S(1)}, u32[]{:S(2)}, u32[]{:S(2)}) collective-permute-start(bf16[2,128,1024]{2,1,0:T(8,128)(2,1)S(1)} %pad_maximum_fusion.near_ref), channel_id=1, source_target_pairs={{0,8},{1,9},{2,10},{3,11},{4,12},{5,13},{6,14},{7,15},{8,16},{9,17... | collective-permute-start | bytes 1572872 | tf_op jit(solution)/shard_map/ppermute | solution.py:22
  4.7 0.1 pad_add_fusion.5
  4.8 0.1 pad_add_fusion.4
  4.9 0.0 collective-permute-done.1.far_ref
  4.9 0.0 copy-start
  4.9 1.6 %copy-done = bf16[128,8192]{1,0:T(8,128)(2,1)S(1)} copy-done((bf16[128,8192]{1,0:T(8,128)(2,1)S(1)}, bf16[128,8192]{1,0:T(8,128)(2,1)}, u32[]{:S(2)}) %copy-start) | copy-done | bytes 2097176
  6.5 0.0 copy-start.1
  6.5 0.7 %copy-done.1 = s32[12]{0:T(128)S(1)} copy-done((s32[12]{0:T(128)S(1)}, s32[12]{0:T(128)}, u32[]{:S(2)}) %copy-start.1) | copy-done | bytes 72
  7.1 4.8 %attend_own.1 = (bf16[128,8192]{1,0:T(8,128)(2,1)S(1)}, f32[8,8192]{1,0:T(8,128)S(1)}, f32[144,8192]{1,0:T(8,128)S(1)}) custom-call(s32[4]{0:T(128)S(1)} %get-tuple-element.48.place_ref, s32[12]{0:T(128)S(1)} %copy-done.1, bf16[128,8192]{1,0:T(8,128)(2,1)S(1)} %copy-done, bf16[2,128,1024]{2,1,0:T(8,128)(2,1)S(1)} %pad_maximum_fusion.near_ref, ...), custom_call_target="tpu_custom_call" | custom-call | tf_op jit(solution)/shard_map/attend_own/pallas_call | solution.py:204
  11.9 5.5 %collective-permute-done.near_ref = bf16[2,128,1024]{2,1,0:T(8,128)(2,1)S(1)} collective-permute-done((bf16[2,128,1024]{2,1,0:T(8,128)(2,1)S(1)}, bf16[2,128,1024]{2,1,0:T(8,128)(2,1)S(1)}, u32[]{:S(2)}, u32[]{:S(2)}) %collective-permute-start) | collective-permute-done | bytes 524320 | tf_op jit(solution)/shard_map/ppermute | solution.py:22
  17.4 0.0 collective-permute-start.5
  17.4 1.1 %broadcast_select_fusion = (bf16[2,128,1024]{2,1,0:T(8,128)(2,1)S(1)}, bf16[2,128,1024]{2,1,0:T(8,128)(2,1)S(1)}, bf16[2,128,1024]{2,1,0:T(8,128)(2,1)S(1)}) fusion(bf16[2,128,1024]{2,1,0:T(8,128)(2,1)S(1)} %collective-permute-done.near_ref, pred[]{:T(512)S(6)} %gt.8, bf16[1,128,1024]{2,1,0:T(8,128)(2,1)} %bitcast.14, bf16[1,128,1024]{2,1,0:T(8,128)(2,1)} %bitcast.16, ...), kind=kLoop, calls=%fused_computation.1 | loop fusion | flops 1048576 | bytes 2621443 | tf_op jit(solution)/shard_map/jit(_where)/select_n | solution.py:219
  18.5 1.6 %collective-permute-start.4 = (bf16[2,128,1024]{2,1,0:T(8,128)(2,1)S(1)}, bf16[2,128,1024]{2,1,0:T(8,128)(2,1)S(1)}, u32[]{:S(2)}, u32[]{:S(2)}) collective-permute-start(bf16[2,128,1024]{2,1,0:T(8,128)(2,1)S(1)} %get-tuple-element.43), channel_id=1, source_target_pairs={{0,2},{1,5},{2,0},{3,7},{4,6},{5,1},{6,4},{7,3},{8,10},{9,13},{10,... | collective-permute-start | bytes 1572872 | tf_op jit(solution)/shard_map/ppermute | solution.py:31
  20.1 0.0 collective-permute-done.5.far_ref
  20.1 5.9 %attend_span.3 = (f32[8,8192]{1,0:T(8,128)S(1)}, f32[144,8192]{1,0:T(8,128)S(1)}) custom-call(s32[4]{0:T(128)S(1)} %get-tuple-element.41.place_ref, s32[12]{0:T(128)S(1)} %copy-done.1, bf16[2,128,1024]{2,1,0:T(8,128)(2,1)S(1)} %collective-permute-done.near_ref, ...), custom_call_target="tpu_custom_call", output_to_operand_aliasing={{0}: (5, {}), {1}: (6, {})} | custom-call | tf_op jit(solution)/shard_map/attend_span/pallas_call | solution.py:234
  26.0 1.8 %collective-permute-done.4.near_ref = bf16[2,128,1024]{2,1,0:T(8,128)(2,1)S(1)} collective-permute-done((bf16[2,128,1024]{2,1,0:T(8,128)(2,1)S(1)}, bf16[2,128,1024]{2,1,0:T(8,128)(2,1)S(1)}, u32[]{:S(2)}, u32[]{:S(2)}) %collective-permute-start.4) | collective-permute-done | bytes 524320 | tf_op jit(solution)/shard_map/ppermute | solution.py:31
  27.8 0.0 collective-permute-start.6
  27.8 1.5 %collective-permute-start.3 = (bf16[2,128,1024]{2,1,0:T(8,128)(2,1)S(1)}, bf16[2,128,1024]{2,1,0:T(8,128)(2,1)S(1)}, u32[]{:S(2)}, u32[]{:S(2)}) collective-permute-start(bf16[2,128,1024]{2,1,0:T(8,128)(2,1)S(1)} %get-tuple-element.44), channel_id=1, source_target_pairs={{0,4},{1,3},{2,6},{3,1},{4,0},{5,7},{6,2},{7,5},{8,12},{9,11},{10,... | collective-permute-start | bytes 1572872 | tf_op jit(solution)/shard_map/ppermute | solution.py:31
  29.3 0.4 collective-permute-done.6.far_ref
  29.7 5.9 %attend_span.4 = (f32[8,8192]{1,0:T(8,128)S(1)}, f32[144,8192]{1,0:T(8,128)S(1)}) custom-call(s32[4]{0:T(128)S(1)} %get-tuple-element.46.place_ref, s32[12]{0:T(128)S(1)} %copy-done.1, bf16[2,128,1024]{2,1,0:T(8,128)(2,1)S(1)} %collective-permute-done.4.near_ref, ...), custom_call_target="tpu_custom_call", output_to_operand_aliasing={{0}: (5, {}), {1}: (6, {})} | custom-call | tf_op jit(solution)/shard_map/attend_span/pallas_call | solution.py:234
  35.6 1.3 %collective-permute-done.3.near_ref = bf16[2,128,1024]{2,1,0:T(8,128)(2,1)S(1)} collective-permute-done((bf16[2,128,1024]{2,1,0:T(8,128)(2,1)S(1)}, bf16[2,128,1024]{2,1,0:T(8,128)(2,1)S(1)}, u32[]{:S(2)}, u32[]{:S(2)}) %collective-permute-start.3) | collective-permute-done | bytes 524320 | tf_op jit(solution)/shard_map/ppermute | solution.py:31
  36.9 0.0 collective-permute-start.7
  36.9 2.4 %collective-permute-start.2 = (bf16[2,128,1024]{2,1,0:T(8,128)(2,1)S(1)}, bf16[2,128,1024]{2,1,0:T(8,128)(2,1)S(1)}, u32[]{:S(2)}, u32[]{:S(2)}) collective-permute-start(bf16[2,128,1024]{2,1,0:T(8,128)(2,1)S(1)} %get-tuple-element.45), channel_id=1, source_target_pairs={{0,6},{1,7},{2,4},{3,5},{4,2},{5,3},{6,0},{7,1},{8,14},{9,15},{10,... | collective-permute-start | bytes 1572872 | tf_op jit(solution)/shard_map/ppermute | solution.py:31
  39.4 0.0 collective-permute-done.7.far_ref
  39.4 5.9 %attend_span.5 = (f32[8,8192]{1,0:T(8,128)S(1)}, f32[144,8192]{1,0:T(8,128)S(1)}) custom-call(s32[4]{0:T(128)S(1)} %get-tuple-element.47.place_ref, s32[12]{0:T(128)S(1)} %copy-done.1, bf16[2,128,1024]{2,1,0:T(8,128)(2,1)S(1)} %collective-permute-done.3.near_ref, ...), custom_call_target="tpu_custom_call", output_to_operand_aliasing={{0}: (5, {}), {1}: (6, {})} | custom-call | tf_op jit(solution)/shard_map/attend_span/pallas_call | solution.py:234
  45.3 6.8 %collective-permute-done.2.near_ref = bf16[2,128,1024]{2,1,0:T(8,128)(2,1)S(1)} collective-permute-done((bf16[2,128,1024]{2,1,0:T(8,128)(2,1)S(1)}, bf16[2,128,1024]{2,1,0:T(8,128)(2,1)S(1)}, u32[]{:S(2)}, u32[]{:S(2)}) %collective-permute-start.2) | collective-permute-done | bytes 524320 | tf_op jit(solution)/shard_map/ppermute | solution.py:31
  52.2 0.0 collective-permute-start.8
  52.2 1.9 %collective-permute-done.8.far_ref = bf16[2,128,1024]{2,1,0:T(8,128)(2,1)S(1)} collective-permute-done((bf16[2,128,1024]{2,1,0:T(8,128)(2,1)S(1)}, bf16[2,128,1024]{2,1,0:T(8,128)(2,1)S(1)}, u32[]{:S(2)}, u32[]{:S(2)}) %collective-permute-start.8) | collective-permute-done | bytes 524320 | tf_op jit(solution)/shard_map/ppermute | solution.py:36
  54.1 8.3 %attend_last.1 = (bf16[128,8192]{1,0:T(8,128)(2,1)}, f32[8,8192]{1,0:T(8,128)S(1)}, f32[144,8192]{1,0:T(8,128)S(1)}) custom-call(s32[4]{0:T(128)S(1)} %get-tuple-element.49.place_ref, s32[12]{0:T(128)S(1)} %copy-done.1, bf16[2,128,1024]{2,1,0:T(8,128)(2,1)S(1)} %collective-permute-done.2.near_ref, ...), custom_call_target="tpu_custom_call", output_to_operand_aliasing={{1}: (5, {}), {2}: (6, {})} | custom-call | tf_op jit(solution)/shard_map/attend_last/pallas_call | solution.py:234
Async XLA Ops:
  1.1 3.8 %collective-permute-start.1 = (bf16[2,128,1024]{2,1,0:T(8,128)(2,1)S(1)}, bf16[2,128,1024]{2,1,0:T(8,128)(2,1)S(1)}, u32[]{:S(2)}, u32[]{:S(2)}) collective-permute-start(bf16[2,128,1024]{2,1,0:T(8,128)(2,1)S(1)} %pad_maximum_fusion.near_ref), channel_id=1, source_target_pairs={{0,1},{1,0},{2,3},{3,2},{4,5},{5,4},{6,7},{7,6},{8,9},{9,8},{10,11... | collective-permute-start | bytes 1572872 | tf_op jit(solution)/shard_map/ppermute | solution.py:36
  1.2 16.2 %collective-permute-start = (bf16[2,128,1024]{2,1,0:T(8,128)(2,1)S(1)}, bf16[2,128,1024]{2,1,0:T(8,128)(2,1)S(1)}, u32[]{:S(2)}, u32[]{:S(2)}) collective-permute-start(bf16[2,128,1024]{2,1,0:T(8,128)(2,1)S(1)} %pad_maximum_fusion.near_ref), channel_id=1, source_target_pairs={{0,8},{1,9},{2,10},{3,11},{4,12},{5,13},{6,14},{7,15},{8,16},{9,17... | collective-permute-start | bytes 1572872 | tf_op jit(solution)/shard_map/ppermute | solution.py:22
  4.9 1.6 %copy-start = (bf16[128,8192]{1,0:T(8,128)(2,1)S(1)}, bf16[128,8192]{1,0:T(8,128)(2,1)}, u32[]{:S(2)}) copy-start(bf16[128,8192]{1,0:T(8,128)(2,1)} %q_ref.1) | copy-start | bytes 6291460
  6.5 0.7 %copy-start.1 = (s32[12]{0:T(128)S(1)}, s32[12]{0:T(128)}, u32[]{:S(2)}) copy-start(s32[12]{0:T(128)} %lengths_ref.9) | copy-start | bytes 148
  17.4 2.7 %collective-permute-start.5 = (bf16[2,128,1024]{2,1,0:T(8,128)(2,1)S(1)}, bf16[2,128,1024]{2,1,0:T(8,128)(2,1)S(1)}, u32[]{:S(2)}, u32[]{:S(2)}) collective-permute-start(bf16[2,128,1024]{2,1,0:T(8,128)(2,1)S(1)} %collective-permute-done.near_ref), channel_id=1, source_target_pairs={{0,1},{1,0},{2,3},{3,2},{4,5},{5,4},{6,7},{7,6},{8,9},{9,8},{10,11... | collective-permute-start | bytes 1572872 | tf_op jit(solution)/shard_map/ppermute | solution.py:36
  18.5 9.2 %collective-permute-start.4 = (bf16[2,128,1024]{2,1,0:T(8,128)(2,1)S(1)}, bf16[2,128,1024]{2,1,0:T(8,128)(2,1)S(1)}, u32[]{:S(2)}, u32[]{:S(2)}) collective-permute-start(bf16[2,128,1024]{2,1,0:T(8,128)(2,1)S(1)} %get-tuple-element.43), channel_id=1, source_target_pairs={{0,2},{1,5},{2,0},{3,7},{4,6},{5,1},{6,4},{7,3},{8,10},{9,13},{10,... | collective-permute-start | bytes 1572872 | tf_op jit(solution)/shard_map/ppermute | solution.py:31
  27.8 1.9 %collective-permute-start.6 = (bf16[2,128,1024]{2,1,0:T(8,128)(2,1)S(1)}, bf16[2,128,1024]{2,1,0:T(8,128)(2,1)S(1)}, u32[]{:S(2)}, u32[]{:S(2)}) collective-permute-start(bf16[2,128,1024]{2,1,0:T(8,128)(2,1)S(1)} %collective-permute-done.4.near_ref), channel_id=1, source_target_pairs={{0,1},{1,0},{2,3},{3,2},{4,5},{5,4},{6,7},{7,6},{8,9},{9,8},{10,11... | collective-permute-start | bytes 1572872 | tf_op jit(solution)/shard_map/ppermute | solution.py:36
  27.8 9.2 %collective-permute-start.3 = (bf16[2,128,1024]{2,1,0:T(8,128)(2,1)S(1)}, bf16[2,128,1024]{2,1,0:T(8,128)(2,1)S(1)}, u32[]{:S(2)}, u32[]{:S(2)}) collective-permute-start(bf16[2,128,1024]{2,1,0:T(8,128)(2,1)S(1)} %get-tuple-element.44), channel_id=1, source_target_pairs={{0,4},{1,3},{2,6},{3,1},{4,0},{5,7},{6,2},{7,5},{8,12},{9,11},{10,... | collective-permute-start | bytes 1572872 | tf_op jit(solution)/shard_map/ppermute | solution.py:31
  36.9 2.5 %collective-permute-start.7 = (bf16[2,128,1024]{2,1,0:T(8,128)(2,1)S(1)}, bf16[2,128,1024]{2,1,0:T(8,128)(2,1)S(1)}, u32[]{:S(2)}, u32[]{:S(2)}) collective-permute-start(bf16[2,128,1024]{2,1,0:T(8,128)(2,1)S(1)} %collective-permute-done.3.near_ref), channel_id=1, source_target_pairs={{0,1},{1,0},{2,3},{3,2},{4,5},{5,4},{6,7},{7,6},{8,9},{9,8},{10,11... | collective-permute-start | bytes 1572872 | tf_op jit(solution)/shard_map/ppermute | solution.py:36
  36.9 15.2 %collective-permute-start.2 = (bf16[2,128,1024]{2,1,0:T(8,128)(2,1)S(1)}, bf16[2,128,1024]{2,1,0:T(8,128)(2,1)S(1)}, u32[]{:S(2)}, u32[]{:S(2)}) collective-permute-start(bf16[2,128,1024]{2,1,0:T(8,128)(2,1)S(1)} %get-tuple-element.45), channel_id=1, source_target_pairs={{0,6},{1,7},{2,4},{3,5},{4,2},{5,3},{6,0},{7,1},{8,14},{9,15},{10,... | collective-permute-start | bytes 1572872 | tf_op jit(solution)/shard_map/ppermute | solution.py:31
  52.2 1.9 %collective-permute-start.8 = (bf16[2,128,1024]{2,1,0:T(8,128)(2,1)S(1)}, bf16[2,128,1024]{2,1,0:T(8,128)(2,1)S(1)}, u32[]{:S(2)}, u32[]{:S(2)}) collective-permute-start(bf16[2,128,1024]{2,1,0:T(8,128)(2,1)S(1)} %collective-permute-done.2.near_ref), channel_id=1, source_target_pairs={{0,1},{1,0},{2,3},{3,2},{4,5},{5,4},{6,7},{7,6},{8,9},{9,8},{10,11... | collective-permute-start | bytes 1572872 | tf_op jit(solution)/shard_map/ppermute | solution.py:36

commit v4 on v3

v4 whole, which is shorter than its diff:
```python
import functools
import math

import jax
import jax.numpy as jnp
from jax import lax
from jax.experimental import pallas as pl
from jax.experimental.pallas import tpu as pltpu
from jax.sharding import PartitionSpec as P

HD = 128
REACH = 4
NEVER = -1e30
SCORE_SCALE = HD ** (-0.5) * math.log2(math.e)
SUM_ROWS = 16
AXES = ("ctx", "head")
PARTNER = ((1, 2), (2, 1))
SAFE = 100.0


def to_next_group(block):
    spans, cores = lax.axis_size("ctx"), lax.axis_size("head")
    pairs = [(s * cores + h, (s + REACH) * cores + h) for s in range(spans - REACH) for h in range(cores)]
    return lax.ppermute(block, AXES, pairs)


def to_opposite(block):
    spans, cores = lax.axis_size("ctx"), lax.axis_size("head")
    pairs = []
    for s in range(spans):
        place = s % REACH
        target = s - place + REACH - 1 - place
        target += 0 if target > s else REACH
        if target < spans:
            pairs += [(s * cores + h, target * cores + h) for h in range(cores)]
    return lax.ppermute(block, AXES, pairs)


def in_group(block, turn):
    spans, cores = lax.axis_size("ctx"), lax.axis_size("head")
    pairs = []
    for s in range(spans):
        for h in range(cores):
            pairs.append((s * cores + h, (s ^ PARTNER[h][turn]) * cores + h))
    return lax.ppermute(block, AXES, pairs)


def to_other_core(block):
    cores = lax.axis_size("head")
    return lax.ppermute(block, "head", [(h, cores - 1 - h) for h in range(cores)])


def doc_starts(lengths_ref, first, last):
    def one_doc(i, carry):
        start, lo_first, lo_last = carry
        start = start + lengths_ref[i]
        return start, jnp.where(start <= first, start, lo_first), jnp.where(start <= last, start, lo_last)

    zero = jnp.int32(0)
    _, lo_first, lo_last = lax.fori_loop(0, lengths_ref.shape[0], one_doc, (zero, zero, zero))
    return lo_first, lo_last


def doc_start_rows(lengths_ref, first_query, rows):
    pos = first_query + lax.broadcasted_iota(jnp.int32, (8, rows), 1)

    def one_doc(i, carry):
        start, lo = carry
        start = start + lengths_ref[i]
        return start, jnp.where(start <= pos, start, lo)

    zero = jnp.zeros((8, rows), jnp.int32)
    return lax.fori_loop(0, lengths_ref.shape[0], one_doc, (jnp.int32(0), zero))[1]


def head_group(g, width):
    return pl.ds(pl.multiple_of(g * width, width), width)


def positions(start, keys, queries):
    return start + lax.broadcasted_iota(jnp.int32, (keys, queries), 0)


def score_bound(blocks, q_square):
    largest = None
    for block in blocks:
        top = jnp.max(jnp.abs(block[0].astype(jnp.float32)), axis=0, keepdims=True)
        largest = top if largest is None else jnp.maximum(largest, top)
    square = largest * largest
    kv_heads = square.shape[1] // HD
    by_head = jnp.concatenate([square[:, g * HD : (g + 1) * HD] for g in range(kv_heads)], axis=0)
    return jnp.max(jnp.sum(by_head, axis=1, keepdims=True) * q_square)


def is_safe(bound):
    return bound * (SCORE_SCALE * SCORE_SCALE) <= SAFE * SAFE


def absorb(key_block, value_block, allowed, state, at, initial, shifted, group_size):
    qt_ref, max_ref, acc_ref = state
    keys = key_block.shape[0]
    widened = jnp.concatenate([value_block.T, jnp.ones((SUM_ROWS, keys), value_block.dtype)], axis=0)
    scores = jnp.dot(key_block, qt_ref[:, at], preferred_element_type=jnp.float32)
    if allowed is not None:
        allowed = jnp.concatenate([allowed] * group_size, axis=1)
    if shifted:
        if allowed is not None:
            scores = jnp.where(allowed, scores, NEVER)
        max_new = jnp.max(scores, axis=0, keepdims=True)
        if not initial:
            max_old = max_ref[:1, at]
            max_new = jnp.maximum(max_old, max_new)
        weights = jnp.exp2((scores - max_new) * SCORE_SCALE)
        max_ref[:, at] = jnp.broadcast_to(max_new, (8, max_new.shape[1]))
    else:
        weights = jnp.exp2(scores * SCORE_SCALE)
        if allowed is not None:
            weights = jnp.where(allowed, weights, 0.0)
        if initial:
            max_ref[:, at] = jnp.zeros((8, scores.shape[1]), jnp.float32)
    added = jnp.dot(widened, weights.astype(jnp.bfloat16), preferred_element_type=jnp.float32)
    if initial:
        acc_ref[:, at] = added
    elif shifted:
        acc_ref[:, at] = acc_ref[:, at] * jnp.exp2((max_old - max_new) * SCORE_SCALE) + added
    else:
        acc_ref[:, at] += added


def own_kernel(
    place_ref, lengths_ref, q_ref, near_ref, far_ref, qt_ref, max_ref, acc_ref, square_ref, safe_ref, *, group_size
):
    rows = q_ref.shape[0]
    width = group_size * rows
    kv_heads = near_ref.shape[2] // HD
    first_query, half = place_ref[0], place_ref[1]
    own_start = first_query - half * rows
    lo_first, _ = doc_starts(lengths_ref, first_query, first_query)
    lo = doc_start_rows(lengths_ref, first_query, rows)
    lo = jnp.concatenate([lo] * (rows // 8), axis=0)
    query_pos = first_query + lax.broadcasted_iota(jnp.int32, (rows, rows), 1)
    key_pos = positions(first_query, rows, rows)
    own_allowed = (key_pos >= lo) & (key_pos <= query_pos)
    far_allowed = positions(own_start, rows, rows) >= lo
    state = (qt_ref, max_ref, acc_ref)

    def turn_queries(g, _):
        q = q_ref[:, head_group(g, group_size * HD)]
        qt = jnp.concatenate([q[:, h * HD : (h + 1) * HD].T for h in range(group_size)], axis=1)
        qt_ref[:, head_group(g, width)] = qt
        wide = qt.astype(jnp.float32)
        square = jnp.max(jnp.sum(wide * wide, axis=0, keepdims=True), axis=1, keepdims=True)
        square_ref[pl.ds(g, 1), :] = jnp.broadcast_to(square, (1, HD))
        return 0

    lax.fori_loop(0, kv_heads, turn_queries, 0)
    safe = is_safe(score_bound([near_ref, far_ref], square_ref[:, :1]))
    safe_ref[0] = safe.astype(jnp.int32)

    def work(shifted):
        def one_group(g, _):
            at = head_group(g, width)
            kv = head_group(g, HD)
            absorb(near_ref[0, :, kv], near_ref[1, :, kv], own_allowed, state, at, True, shifted, group_size)

            @pl.when((half == 1) & (own_start + rows > lo_first))
            def _():
                absorb(far_ref[0, :, kv], far_ref[1, :, kv], far_allowed, state, at, False, shifted, group_size)

            return 0

        lax.fori_loop(0, kv_heads, one_group, 0)

    pl.when(safe)(lambda: work(False))
    pl.when(jnp.logical_not(safe))(lambda: work(True))


def span_kernel(place_ref, lengths_ref, safe_in, square_ref, *refs, spans, group_size, last):
    blocks, (qt_ref, max_in, acc_in), refs = refs[: 2 * spans], refs[2 * spans : 2 * spans + 3], refs[2 * spans + 3 :]
    del max_in, acc_in
    out_ref = refs[0] if last else None
    max_ref, acc_ref, safe_ref = refs[-3:]
    rows = blocks[0].shape[1]
    width = group_size * rows
    kv_heads = blocks[0].shape[2] // HD
    first_query = place_ref[0]
    lo_first, lo_last = doc_starts(lengths_ref, first_query, first_query + rows - 1)
    state = (qt_ref, max_ref, acc_ref)
    safe_ref[0] = safe_in[0]

    def span(near_ref, far_ref, near_start, far_start, masked, shifted):
        allowed = None
        if masked:
            lo = jnp.concatenate([doc_start_rows(lengths_ref, first_query, rows)] * (rows // 4), axis=0)
            key_pos = jnp.concatenate([positions(near_start, rows, rows), positions(far_start, rows, rows)], axis=0)
            allowed = key_pos >= lo

        def one_group(g, _):
            kv = head_group(g, HD)
            absorb(
                jnp.concatenate([near_ref[0, :, kv], far_ref[0, :, kv]], axis=0),
                jnp.concatenate([near_ref[1, :, kv], far_ref[1, :, kv]], axis=0),
                allowed,
                state,
                head_group(g, width),
                False,
                shifted,
                group_size,
            )
            return 0

        lax.fori_loop(0, kv_heads, one_group, 0)

    for number in range(spans):
        near_ref, far_ref = blocks[2 * number : 2 * number + 2]
        near_start, far_start = place_ref[2 + 2 * number], place_ref[3 + 2 * number]
        work = functools.partial(span, near_ref, far_ref, near_start, far_start)
        needed = jnp.maximum(near_start, far_start) + rows > lo_first
        whole = jnp.minimum(near_start, far_start) >= lo_last

        @pl.when(needed)
        def _():
            safe = (safe_ref[0] == 1) & is_safe(score_bound([near_ref, far_ref], square_ref[:, :1]))
            safe_ref[0] = safe.astype(jnp.int32)
            pl.when(safe & whole)(lambda: work(False, False))
            pl.when(safe & jnp.logical_not(whole))(lambda: work(True, False))
            pl.when(jnp.logical_not(safe))(lambda: work(True, True))

    if last:

        def finish(g, _):
            acc = acc_ref[:, head_group(g, width)]
            finished = (acc[:HD] * (1.0 / acc[HD : HD + 1])).astype(jnp.bfloat16)
            out_ref[:, head_group(g, group_size * HD)] = jnp.concatenate(
                [finished[:, h * rows : (h + 1) * rows].T for h in range(group_size)], axis=1
            )
            return 0

        lax.fori_loop(0, kv_heads, finish, 0)


def per_device(queries, keys, values, doc_lengths):
    rows = queries.shape[0]
    kv_heads = keys.shape[1] // HD
    group_size = queries.shape[1] // keys.shape[1]
    head_rows = (queries.shape[1] // HD) * rows
    half, span = lax.axis_index("head"), lax.axis_index("ctx")
    cores = lax.axis_size("head")
    place_in_group = lax.rem(span, REACH)
    first_query = (span * cores + half) * rows

    vmem = pl.BlockSpec(memory_space=pltpu.VMEM)
    smem = pl.BlockSpec(memory_space=pltpu.SMEM)
    qt_shape = jax.ShapeDtypeStruct((HD, head_rows), queries.dtype)
    max_shape = jax.ShapeDtypeStruct((8, head_rows), jnp.float32)
    acc_shape = jax.ShapeDtypeStruct((HD + SUM_ROWS, head_rows), jnp.float32)
    square_shape = jax.ShapeDtypeStruct((kv_heads, HD), jnp.float32)
    safe_shape = jax.ShapeDtypeStruct((1,), jnp.int32)
    params = pltpu.CompilerParams(vmem_limit_bytes=24 * 1024 * 1024)
    cost = pl.CostEstimate(flops=0, bytes_accessed=0, transcendentals=0)

    def place(*spans_of):
        parts = [first_query, half]
        for near_span, far_span in spans_of:
            parts += [(near_span * cores + half) * rows, (far_span * cores + 1 - half) * rows]
        return jnp.stack(parts).astype(jnp.int32)

    own = jnp.stack([keys, values])
    behind = to_next_group(own)
    opposite = to_opposite(own)
    own_far = to_other_core(own)

    qt, row_max, acc, square, safe = pl.pallas_call(
        functools.partial(own_kernel, group_size=group_size),
        in_specs=[smem, smem, vmem, vmem, vmem],
        out_specs=(vmem, vmem, vmem, vmem, smem),
        out_shape=(qt_shape, max_shape, acc_shape, square_shape, safe_shape),
        compiler_params=params,
        cost_estimate=cost,
        name="attend_own",
    )(place(), doc_lengths, queries, own, own_far)

    def source(partner):
        from_place = place_in_group ^ partner
        return span - place_in_group + from_place - jnp.where(from_place > place_in_group, REACH, 0)

    def attend(state, arrivals, last):
        safe, row_max, acc = state
        out_shapes = (max_shape, acc_shape, safe_shape)
        if last:
            out_shapes = (jax.ShapeDtypeStruct(queries.shape, queries.dtype),) + out_shapes
        blocks = []
        for _, _, near in arrivals:
            blocks += [near, to_other_core(near)]
        at = 4 + len(blocks)
        *out, row_max, acc, safe = pl.pallas_call(
            functools.partial(span_kernel, spans=len(arrivals), group_size=group_size, last=last),
            in_specs=[smem, smem, smem] + [vmem] * at,
            out_specs=(vmem,) * (len(out_shapes) - 1) + (smem,),
            out_shape=out_shapes,
            input_output_aliases={at + 1: len(out_shapes) - 3, at + 2: len(out_shapes) - 2},
            compiler_params=params,
            cost_estimate=cost,
            name="attend_last" if last else "attend_spans",
        )(place(*[a[:2] for a in arrivals]), doc_lengths, safe, square, *blocks, qt, row_max, acc)
        return out, (safe, row_max, acc)

    behind, opposite, acc = lax.optimization_barrier((behind, opposite, acc))
    exchanged = []
    for turn in range(2):
        mine = jnp.where(half == 0, PARTNER[0][turn], PARTNER[1][turn])
        other = jnp.where(half == 0, PARTNER[1][turn], PARTNER[0][turn])
        send = jnp.where((place_in_group ^ mine) > place_in_group, own, behind)
        exchanged.append((source(mine), source(other), in_group(send, turn)))
    arrivals = [
        (span - REACH, span - REACH, behind),
        (source(REACH - 1), source(REACH - 1), opposite),
    ]
    _, (safe, row_max, acc) = attend((safe, row_max, acc), arrivals, False)
    first, second, acc = lax.optimization_barrier((exchanged[0][2], exchanged[1][2], acc))
    arrivals = [exchanged[0][:2] + (first,), exchanged[1][:2] + (second,)]
    (out,), _ = attend((safe, row_max, acc), arrivals, True)
    return out


def solution(mesh):
    placed = P(AXES, None)
    return jax.shard_map(
        per_device, mesh=mesh, in_specs=(placed, placed, placed, P()), out_specs=placed, check_vma=False
    )
```

time: 63 us -> 73.6 us (1.17)
  waiting for transfers between devices: 17.7 us -> 2.22 us
  local copies, waits for them, and re-layouts: 2.25 us -> 13.2 us
  starting transfers between devices: 9.09 us -> 18.2 us
  Pallas kernels: 30.9 us -> 36.2 us
  other arithmetic: 2.37 us -> 3.25 us
    unnamed x4 -> x18, local copies, waits for them, and re-layouts: 2.25 us -> 13 us
    ppermute x3 -> x2, waiting for transfers between devices: 9.95 us -> 0.01 us  [in_group(): return lax.ppermute(block, AXES, pairs)]
    ppermute x1, waiting for transfers between devices: 5.48 us -> 0.01 us  [to_next_group(): return lax.ppermute(block, AXES, pairs)]
    ppermute x5, starting transfers between devices: 0.08 us -> 4.47 us  [to_other_core(): lax.ppermute(block, 'head', [(h, cores - 1 - h) for h in range(cores)])]
    ppermute x0 -> x1, starting transfers between devices: none -> 4.36 us  [to_opposite(): return lax.ppermute(block, AXES, pairs)]
    pallas_call x4 -> x2, Pallas kernels: 26.1 us -> 29.3 us  [attend(): pl.pallas_call(functools.partial(span_kernel, spans=len(arrivals), group_...]
    pallas_call x1, Pallas kernels: 4.77 us -> 6.88 us  [per_device(): pl.pallas_call(functools.partial(own_kernel, group_size=group_size), in_s...]
    select_n x1, other arithmetic: 1.14 us -> 2.09 us  [per_device(): send = jnp.where(place_in_group ^ mine > place_in_group, own, behind)]
  transfers between devices with their start and end apart: 9 -> 9, of which waited for: 6 -> 2; matrix products, arithmetic and copies ran while one was open for 2% -> 3% of each run, Pallas kernels for 36% -> 28%
where the time goes in v4:
time: 73.6 us; the launch traced here: 73.2 us
  Pallas kernels  36.2 us (49%)
  starting transfers between devices  18.2 us (25%)
  local copies, waits for them, and re-layouts  13.2 us (18%)
  other arithmetic  3.25 us (4%)
  waiting for transfers between devices  2.22 us (3%)
    pallas_call x2, Pallas kernels, attend(): pl.pallas_call(functools.partial(span_kernel, spans=len(arrivals), group_...  29.3 us
    unnamed x18, local copies, waits for them, and re-layouts  13 us
    pallas_call x1, Pallas kernels, per_device(): pl.pallas_call(functools.partial(own_kernel, group_size=group_size), in_s...  6.88 us
    ppermute x2, starting transfers between devices, in_group(): return lax.ppermute(block, AXES, pairs)  5.91 us
    ppermute x5, starting transfers between devices, to_other_core(): lax.ppermute(block, 'head', [(h, cores - 1 - h) for h in range(cores)])  4.47 us
    ppermute x1, starting transfers between devices, to_opposite(): return lax.ppermute(block, AXES, pairs)  4.36 us
    ppermute x1, starting transfers between devices, to_next_group(): return lax.ppermute(block, AXES, pairs)  3.48 us
    ppermute x5, waiting for transfers between devices, to_other_core(): lax.ppermute(block, 'head', [(h, cores - 1 - h) for h in range(cores)])  2.2 us
  transfers between devices with their start and end apart: 9, of which 2 were waited for; matrix products, arithmetic and copies ran while one was open for 3% of the time, Pallas kernels for 28%

profile of v4, /device:TPU:8, one launch (start us, length us, event | category | flops | bytes accessed | tf_op | source)
XLA Modules:
  0.0 73.2 jit_solution(879901905739000951)
XLA Ops:
  0.0 0.0 copy-start.8
  0.0 1.1 %pad_maximum_fusion.near_ref = bf16[2,128,1024]{2,1,0:T(8,128)(2,1)S(1)} fusion(bf16[1,128,1024]{2,1,0:T(8,128)(2,1)} %bitcast.12, bf16[1,128,1024]{2,1,0:T(8,128)(2,1)} %bitcast.14), kind=kLoop, calls=%fused_computation | loop fusion | flops 262144 | bytes 1048576 | tf_op jit(solution)/shard_map/stack | solution.py:268
  1.1 0.1 collective-permute-start
  1.2 4.4 %collective-permute-start.2 = (bf16[2,128,1024]{2,1,0:T(8,128)(2,1)S(1)}, bf16[2,128,1024]{2,1,0:T(8,128)(2,1)}, u32[]{:S(2)}, u32[]{:S(2)}) collective-permute-start(bf16[2,128,1024]{2,1,0:T(8,128)(2,1)S(1)} %pad_maximum_fusion.near_ref), channel_id=1, source_target_pairs={{0,6},{1,7},{2,4},{3,5},{4,10},{5,11},{6,8},{7,9},{8,14},{9,15},{1... | collective-permute-start | bytes 1572872 | tf_op jit(solution)/shard_map/ppermute | solution.py:36
  5.5 3.5 %collective-permute-start.1 = (bf16[2,128,1024]{2,1,0:T(8,128)(2,1)S(1)}, bf16[2,128,1024]{2,1,0:T(8,128)(2,1)S(1)}, u32[]{:S(2)}, u32[]{:S(2)}) collective-permute-start(bf16[2,128,1024]{2,1,0:T(8,128)(2,1)S(1)} %pad_maximum_fusion.near_ref), channel_id=1, source_target_pairs={{0,8},{1,9},{2,10},{3,11},{4,12},{5,13},{6,14},{7,15},{8,16},{9,17... | collective-permute-start | bytes 1572872 | tf_op jit(solution)/shard_map/ppermute | solution.py:24
  9.1 0.1 pad_add_fusion.place_ref
  9.1 0.0 collective-permute-done.far_ref
  9.1 0.0 copy-start.5
  9.1 0.8 %copy-done.5 = bf16[2,128,1024]{2,1,0:T(8,128)(2,1)} copy-done((bf16[2,128,1024]{2,1,0:T(8,128)(2,1)}, bf16[2,128,1024]{2,1,0:T(8,128)(2,1)S(1)}, u32[]{:S(2)}) %copy-start.5) | copy-done | bytes 524312
  9.9 0.0 copy-start.4
  9.9 1.6 %copy-done.4 = bf16[128,8192]{1,0:T(8,128)(2,1)S(1)} copy-done((bf16[128,8192]{1,0:T(8,128)(2,1)S(1)}, bf16[128,8192]{1,0:T(8,128)(2,1)}, u32[]{:S(2)}) %copy-start.4) | copy-done | bytes 2097176
  11.5 0.0 copy-start.6
  11.5 1.0 %copy-done.6 = bf16[2,128,1024]{2,1,0:T(8,128)(2,1)S(1)} copy-done((bf16[2,128,1024]{2,1,0:T(8,128)(2,1)S(1)}, bf16[2,128,1024]{2,1,0:T(8,128)(2,1)}, u32[]{:S(2)}) %copy-start.6) | copy-done | bytes 524312
  12.6 0.0 copy-start.7
  12.6 0.7 copy-done.7
  13.2 6.9 %attend_own.1 = (bf16[128,8192]{1,0:T(8,128)(2,1)S(1)}, f32[8,8192]{1,0:T(8,128)S(1)}, f32[144,8192]{1,0:T(8,128)S(1)}, f32[8,128]{1,0:T(8,128)S(1)}, s32[1]{0:T(128)}) custom-call(s32[2]{0:T(128)S(1)} %pad_add_fusion.place_ref, s32[12]{0:T(128)S(1)} %copy-done.7, bf16[128,8192]{1,0:T(8,128)(2,1)S(1)} %copy-done.4, ...), custom_call_target="tpu_custom_call" | custom-call | tf_op jit(solution)/shard_map/attend_own/pallas_call | solution.py:273
  20.1 0.0 copy-start
  20.1 2.1 %copy-done = f32[144,8192]{1,0:T(8,128)} copy-done((f32[144,8192]{1,0:T(8,128)}, f32[144,8192]{1,0:T(8,128)S(1)}, u32[]{:S(2)}) %copy-start) | copy-done | bytes 4718616
  22.2 0.0 collective-permute-done.2.refs_2_
  22.2 0.0 collective-permute-done.1.refs_0_
  22.2 3.8 %collective-permute-start.4 = (bf16[2,128,1024]{2,1,0:T(8,128)(2,1)}, bf16[2,128,1024]{2,1,0:T(8,128)(2,1)}, u32[]{:S(2)}, u32[]{:S(2)}) collective-permute-start(bf16[2,128,1024]{2,1,0:T(8,128)(2,1)} %collective-permute-done.2.refs_2_), channel_id=1, source_target_pairs={{0,1},{1,0},{2,3},{3,2},{4,5},{5,4},{6,7},{7,6},{8,9},{9,8},{10,11... | collective-permute-start | bytes 1572872 | tf_op jit(solution)/shard_map/ppermute | solution.py:50
  26.1 0.1 collective-permute-start.3
  26.1 2.1 %broadcast_select_fusion = (bf16[2,128,1024]{2,1,0:T(8,128)(2,1)}, bf16[2,128,1024]{2,1,0:T(8,128)(2,1)}) fusion(bf16[2,128,1024]{2,1,0:T(8,128)(2,1)S(1)} %collective-permute-done.1.refs_0_, pred[]{:T(512)S(6)} %gt.7, bf16[1,128,1024]{2,1,0:T(8,128)(2,1)} %bitcast.13, bf16[1,128,1024]{2,1,0:T(8,128)(2,1)} %bitcast.15, pred[]{:T(512)S(6)} %gt.6), kind=kLoop, calls=%fused_computation.1 | loop fusion | flops 786432 | bytes 2097154 | tf_op jit(solution)/shard_map/jit(_where)/select_n | solution.py:313
  28.2 5.4 %collective-permute-start.6 = (bf16[2,128,1024]{2,1,0:T(8,128)(2,1)}, bf16[2,128,1024]{2,1,0:T(8,128)(2,1)S(1)}, u32[]{:S(2)}, u32[]{:S(2)}) collective-permute-start(bf16[2,128,1024]{2,1,0:T(8,128)(2,1)} %get-tuple-element.35), channel_id=1, source_target_pairs={{0,4},{1,3},{2,6},{3,1},{4,0},{5,7},{6,2},{7,5},{8,12},{9,11},{10,... | collective-permute-start | bytes 1572872 | tf_op jit(solution)/shard_map/ppermute | solution.py:45
  33.6 0.5 collective-permute-start.5
  34.1 0.1 stack.63.place_ref
  34.2 0.0 collective-permute-done.4.refs_3_
  34.2 0.0 collective-permute-done.3.refs_1_
  34.2 0.0 copy-done.8
  34.2 0.0 copy-start.1
  34.3 2.3 %copy-done.1 = f32[144,8192]{1,0:T(8,128)S(1)} copy-done((f32[144,8192]{1,0:T(8,128)S(1)}, f32[144,8192]{1,0:T(8,128)}, u32[]{:S(2)}) %copy-start.1) | copy-done | bytes 4718616
  36.6 13.8 %attend_spans.1 = (f32[8,8192]{1,0:T(8,128)S(1)}, f32[144,8192]{1,0:T(8,128)S(1)}, s32[1]{0:T(128)}) custom-call(s32[6]{0:T(128)S(1)} %stack.63.place_ref, s32[12]{0:T(128)S(1)} %copy-done.8, s32[1]{0:T(128)} %get-tuple-element.20.safe_in, f32[8,128]{1,0:T(8,128)S(1)} %get-tuple-element.21.square_ref, ...), custom_call_target="tpu_custom_call", output_to_operand_aliasing={{0}: (9, {}), {1}: (10, {})} | custom-call | tf_op jit(solution)/shard_map/attend_spans/pallas_call | solution.py:296
  50.3 0.0 copy-start.2
  50.4 2.1 %copy-done.2 = f32[144,8192]{1,0:T(8,128)} copy-done((f32[144,8192]{1,0:T(8,128)}, f32[144,8192]{1,0:T(8,128)S(1)}, u32[]{:S(2)}) %copy-start.2) | copy-done | bytes 4718616
  52.5 0.0 collective-permute-done.6.refs_2_
  52.5 0.0 collective-permute-done.5.refs_0_
  52.5 0.0 collective-permute-start.7
  52.5 0.5 collective-permute-start.8
  53.0 0.1 stack.58.place_ref
  53.1 1.6 %collective-permute-done.7.refs_1_ = bf16[2,128,1024]{2,1,0:T(8,128)(2,1)S(1)} collective-permute-done((bf16[2,128,1024]{2,1,0:T(8,128)(2,1)}, bf16[2,128,1024]{2,1,0:T(8,128)(2,1)S(1)}, u32[]{:S(2)}, u32[]{:S(2)}) %collective-permute-start.7) | collective-permute-done | bytes 524320 | tf_op jit(solution)/shard_map/ppermute | solution.py:50
  54.6 0.6 collective-permute-done.8.refs_3_
  55.3 0.0 copy-start.3
  55.3 2.3 %copy-done.3 = f32[144,8192]{1,0:T(8,128)S(1)} copy-done((f32[144,8192]{1,0:T(8,128)S(1)}, f32[144,8192]{1,0:T(8,128)}, u32[]{:S(2)}) %copy-start.3) | copy-done | bytes 4718616
  57.6 15.5 %attend_last.1 = (bf16[128,8192]{1,0:T(8,128)(2,1)}, f32[8,8192]{1,0:T(8,128)S(1)}, f32[144,8192]{1,0:T(8,128)S(1)}, s32[1]{0:T(128)}) custom-call(s32[6]{0:T(128)S(1)} %stack.58.place_ref, s32[12]{0:T(128)S(1)} %copy-done.8, s32[1]{0:T(128)} %get-tuple-element.28.safe_in, ...), custom_call_target="tpu_custom_call", output_to_operand_aliasing={{1}: (9, {}), {2}: (10, {})} | custom-call | tf_op jit(solution)/shard_map/attend_last/pallas_call | solution.py:296
Async XLA Ops:
  0.0 34.2 %copy-start.8 = (s32[12]{0:T(128)S(1)}, s32[12]{0:T(128)}, u32[]{:S(2)}) copy-start(s32[12]{0:T(128)} %lengths_ref.5) | copy-start | bytes 148
  1.1 8.0 %collective-permute-start = (bf16[2,128,1024]{2,1,0:T(8,128)(2,1)S(1)}, bf16[2,128,1024]{2,1,0:T(8,128)(2,1)S(1)}, u32[]{:S(2)}, u32[]{:S(2)}) collective-permute-start(bf16[2,128,1024]{2,1,0:T(8,128)(2,1)S(1)} %pad_maximum_fusion.near_ref), channel_id=1, source_target_pairs={{0,1},{1,0},{2,3},{3,2},{4,5},{5,4},{6,7},{7,6},{8,9},{9,8},{10,11... | collective-permute-start | bytes 1572872 | tf_op jit(solution)/shard_map/ppermute | solution.py:50
  1.2 21.1 %collective-permute-start.2 = (bf16[2,128,1024]{2,1,0:T(8,128)(2,1)S(1)}, bf16[2,128,1024]{2,1,0:T(8,128)(2,1)}, u32[]{:S(2)}, u32[]{:S(2)}) collective-permute-start(bf16[2,128,1024]{2,1,0:T(8,128)(2,1)S(1)} %pad_maximum_fusion.near_ref), channel_id=1, source_target_pairs={{0,6},{1,7},{2,4},{3,5},{4,10},{5,11},{6,8},{7,9},{8,14},{9,15},{1... | collective-permute-start | bytes 1572872 | tf_op jit(solution)/shard_map/ppermute | solution.py:36
  5.5 16.7 %collective-permute-start.1 = (bf16[2,128,1024]{2,1,0:T(8,128)(2,1)S(1)}, bf16[2,128,1024]{2,1,0:T(8,128)(2,1)S(1)}, u32[]{:S(2)}, u32[]{:S(2)}) collective-permute-start(bf16[2,128,1024]{2,1,0:T(8,128)(2,1)S(1)} %pad_maximum_fusion.near_ref), channel_id=1, source_target_pairs={{0,8},{1,9},{2,10},{3,11},{4,12},{5,13},{6,14},{7,15},{8,16},{9,17... | collective-permute-start | bytes 1572872 | tf_op jit(solution)/shard_map/ppermute | solution.py:24
  9.1 0.8 %copy-start.5 = (bf16[2,128,1024]{2,1,0:T(8,128)(2,1)}, bf16[2,128,1024]{2,1,0:T(8,128)(2,1)S(1)}, u32[]{:S(2)}) copy-start(bf16[2,128,1024]{2,1,0:T(8,128)(2,1)S(1)} %collective-permute-done.far_ref) | copy-start | bytes 1572868
  9.9 1.6 %copy-start.4 = (bf16[128,8192]{1,0:T(8,128)(2,1)S(1)}, bf16[128,8192]{1,0:T(8,128)(2,1)}, u32[]{:S(2)}) copy-start(bf16[128,8192]{1,0:T(8,128)(2,1)} %q_ref.1) | copy-start | bytes 6291460
  11.5 1.0 %copy-start.6 = (bf16[2,128,1024]{2,1,0:T(8,128)(2,1)S(1)}, bf16[2,128,1024]{2,1,0:T(8,128)(2,1)}, u32[]{:S(2)}) copy-start(bf16[2,128,1024]{2,1,0:T(8,128)(2,1)} %copy-done.5) | copy-start | bytes 1572868
  12.6 0.7 copy-start.7
  20.1 2.1 %copy-start = (f32[144,8192]{1,0:T(8,128)}, f32[144,8192]{1,0:T(8,128)S(1)}, u32[]{:S(2)}) copy-start(f32[144,8192]{1,0:T(8,128)S(1)} %get-tuple-element.27.refs_6_) | copy-start | bytes 14155780
  22.2 12.0 %collective-permute-start.4 = (bf16[2,128,1024]{2,1,0:T(8,128)(2,1)}, bf16[2,128,1024]{2,1,0:T(8,128)(2,1)}, u32[]{:S(2)}, u32[]{:S(2)}) collective-permute-start(bf16[2,128,1024]{2,1,0:T(8,128)(2,1)} %collective-permute-done.2.refs_2_), channel_id=1, source_target_pairs={{0,1},{1,0},{2,3},{3,2},{4,5},{5,4},{6,7},{7,6},{8,9},{9,8},{10,11... | collective-permute-start | bytes 1572872 | tf_op jit(solution)/shard_map/ppermute | solution.py:50
  26.1 8.2 %collective-permute-start.3 = (bf16[2,128,1024]{2,1,0:T(8,128)(2,1)S(1)}, bf16[2,128,1024]{2,1,0:T(8,128)(2,1)}, u32[]{:S(2)}, u32[]{:S(2)}) collective-permute-start(bf16[2,128,1024]{2,1,0:T(8,128)(2,1)S(1)} %collective-permute-done.1.refs_0_), channel_id=1, source_target_pairs={{0,1},{1,0},{2,3},{3,2},{4,5},{5,4},{6,7},{7,6},{8,9},{9,8},{10,11... | collective-permute-start | bytes 1572872 | tf_op jit(solution)/shard_map/ppermute | solution.py:50
  28.2 24.3 %collective-permute-start.6 = (bf16[2,128,1024]{2,1,0:T(8,128)(2,1)}, bf16[2,128,1024]{2,1,0:T(8,128)(2,1)S(1)}, u32[]{:S(2)}, u32[]{:S(2)}) collective-permute-start(bf16[2,128,1024]{2,1,0:T(8,128)(2,1)} %get-tuple-element.35), channel_id=1, source_target_pairs={{0,4},{1,3},{2,6},{3,1},{4,0},{5,7},{6,2},{7,5},{8,12},{9,11},{10,... | collective-permute-start | bytes 1572872 | tf_op jit(solution)/shard_map/ppermute | solution.py:45
  33.6 18.9 %collective-permute-start.5 = (bf16[2,128,1024]{2,1,0:T(8,128)(2,1)}, bf16[2,128,1024]{2,1,0:T(8,128)(2,1)}, u32[]{:S(2)}, u32[]{:S(2)}) collective-permute-start(bf16[2,128,1024]{2,1,0:T(8,128)(2,1)} %get-tuple-element.36), channel_id=1, source_target_pairs={{0,2},{1,5},{2,0},{3,7},{4,6},{5,1},{6,4},{7,3},{8,10},{9,13},{10,... | collective-permute-start | bytes 1572872 | tf_op jit(solution)/shard_map/ppermute | solution.py:45
  34.2 2.3 %copy-start.1 = (f32[144,8192]{1,0:T(8,128)S(1)}, f32[144,8192]{1,0:T(8,128)}, u32[]{:S(2)}) copy-start(f32[144,8192]{1,0:T(8,128)} %copy-done) | copy-start | bytes 14155780
  50.3 2.1 %copy-start.2 = (f32[144,8192]{1,0:T(8,128)}, f32[144,8192]{1,0:T(8,128)S(1)}, u32[]{:S(2)}) copy-start(f32[144,8192]{1,0:T(8,128)S(1)} %get-tuple-element.33.refs_6_) | copy-start | bytes 14155780
  52.5 2.2 %collective-permute-start.7 = (bf16[2,128,1024]{2,1,0:T(8,128)(2,1)}, bf16[2,128,1024]{2,1,0:T(8,128)(2,1)S(1)}, u32[]{:S(2)}, u32[]{:S(2)}) collective-permute-start(bf16[2,128,1024]{2,1,0:T(8,128)(2,1)} %collective-permute-done.5.refs_0_), channel_id=1, source_target_pairs={{0,1},{1,0},{2,3},{3,2},{4,5},{5,4},{6,7},{7,6},{8,9},{9,8},{10,11... | collective-permute-start | bytes 1572872 | tf_op jit(solution)/shard_map/ppermute | solution.py:50
  52.5 2.8 %collective-permute-start.8 = (bf16[2,128,1024]{2,1,0:T(8,128)(2,1)S(1)}, bf16[2,128,1024]{2,1,0:T(8,128)(2,1)}, u32[]{:S(2)}, u32[]{:S(2)}) collective-permute-start(bf16[2,128,1024]{2,1,0:T(8,128)(2,1)S(1)} %collective-permute-done.6.refs_2_), channel_id=1, source_target_pairs={{0,1},{1,0},{2,3},{3,2},{4,5},{5,4},{6,7},{7,6},{8,9},{9,8},{10,11... | collective-permute-start | bytes 1572872 | tf_op jit(solution)/shard_map/ppermute | solution.py:50
  55.3 2.3 %copy-start.3 = (f32[144,8192]{1,0:T(8,128)S(1)}, f32[144,8192]{1,0:T(8,128)}, u32[]{:S(2)}) copy-start(f32[144,8192]{1,0:T(8,128)} %copy-done.2) | copy-start | bytes 14155780

commit v5 on v3

v5 whole, which is shorter than its diff:
```python
import functools
import math

import jax
import jax.numpy as jnp
from jax import lax
from jax.experimental import pallas as pl
from jax.experimental.pallas import tpu as pltpu
from jax.sharding import PartitionSpec as P

HD = 128
REACH = 4
NEVER = -1e30
SCORE_SCALE = HD ** (-0.5) * math.log2(math.e)
SUM_ROWS = 16
AXES = ("ctx", "head")
PARTNER = ((1, 2), (2, 1))


def to_next_group(block):
    spans, cores = lax.axis_size("ctx"), lax.axis_size("head")
    pairs = [(s * cores + h, (s + REACH) * cores + h) for s in range(spans - REACH) for h in range(cores)]
    return lax.ppermute(block, AXES, pairs)


def to_opposite(block):
    spans, cores = lax.axis_size("ctx"), lax.axis_size("head")
    pairs = []
    for s in range(spans):
        place = s % REACH
        target = s - place + REACH - 1 - place
        target += 0 if target > s else REACH
        if target < spans:
            pairs += [(s * cores + h, target * cores + h) for h in range(cores)]
    return lax.ppermute(block, AXES, pairs)


def in_group(block, turn):
    spans, cores = lax.axis_size("ctx"), lax.axis_size("head")
    pairs = []
    for s in range(spans):
        for h in range(cores):
            pairs.append((s * cores + h, (s ^ PARTNER[h][turn]) * cores + h))
    return lax.ppermute(block, AXES, pairs)


def to_other_core(block):
    cores = lax.axis_size("head")
    return lax.ppermute(block, "head", [(h, cores - 1 - h) for h in range(cores)])


def doc_starts(lengths_ref, first, last):
    def one_doc(i, carry):
        start, lo_first, lo_last = carry
        start = start + lengths_ref[i]
        return start, jnp.where(start <= first, start, lo_first), jnp.where(start <= last, start, lo_last)

    zero = jnp.int32(0)
    _, lo_first, lo_last = lax.fori_loop(0, lengths_ref.shape[0], one_doc, (zero, zero, zero))
    return lo_first, lo_last


def doc_start_rows(lengths_ref, first_query, keys, rows):
    pos = first_query + lax.broadcasted_iota(jnp.int32, (8, rows), 1)

    def one_doc(i, carry):
        start, lo = carry
        start = start + lengths_ref[i]
        return start, jnp.where(start <= pos, start, lo)

    zero = jnp.zeros((8, rows), jnp.int32)
    lo = lax.fori_loop(0, lengths_ref.shape[0], one_doc, (jnp.int32(0), zero))[1]
    return jnp.concatenate([lo] * (keys // 8), axis=0)


def lanes(at, width):
    return pl.ds(pl.multiple_of(at * width, width), width)


def positions(starts, rows):
    return jnp.concatenate([start + lax.broadcasted_iota(jnp.int32, (rows, rows), 0) for start in starts], axis=0)


def turned(block, count):
    width = block.shape[1] // count
    return jnp.concatenate([block[:, i * width : (i + 1) * width].T for i in range(count)], axis=1)


def absorb(keys, values, allowed, qt, before):
    widened = jnp.concatenate([values.T, jnp.ones((SUM_ROWS, values.shape[0]), values.dtype)], axis=0)
    scores = jnp.dot(keys, qt, preferred_element_type=jnp.float32)
    if allowed is not None:
        allowed = jnp.concatenate([allowed] * (scores.shape[1] // allowed.shape[1]), axis=1)
        scores = jnp.where(allowed, scores, NEVER)
    row_max = jnp.max(scores, axis=0, keepdims=True)
    if before is not None:
        row_max = jnp.maximum(before[0], row_max)
    weights = jnp.exp2((scores - row_max) * SCORE_SCALE).astype(jnp.bfloat16)
    acc = jnp.dot(widened, weights, preferred_element_type=jnp.float32)
    if before is not None:
        acc = before[1] * jnp.exp2((before[0] - row_max) * SCORE_SCALE) + acc
    return row_max, acc


def own_kernel(place_ref, lengths_ref, q_ref, q_far_ref, kv_ref, qt_ref, max_ref, acc_ref, q_near_ref, sem):
    rows, wide = q_far_ref.shape
    kv_heads = kv_ref.shape[3] // HD
    group_size = wide // (kv_heads * HD)
    width = group_size * rows
    half = place_ref[2]
    fetch = pltpu.make_async_copy(q_ref.at[:, lanes(half, wide)], q_near_ref, sem)
    fetch.start()
    starts = place_ref[0], place_ref[1]

    def tokens(side, q_side_ref):
        first = starts[side]
        query_pos = first + lax.broadcasted_iota(jnp.int32, (rows, rows), 1)
        key_pos = positions([first], rows)
        diagonal = (key_pos >= doc_start_rows(lengths_ref, first, rows, rows)) & (key_pos <= query_pos)
        earlier = positions([starts[1 - side]], rows) >= doc_start_rows(lengths_ref, first, rows, rows)

        def one_group(g, _):
            at = lanes(side * kv_heads + g, width)
            kv = lanes(g, HD)
            qt = turned(q_side_ref[:, lanes(g, group_size * HD)], group_size)
            qt_ref[:, at] = qt

            def store(state):
                max_ref[:, at] = jnp.broadcast_to(state[0], (8, width))
                acc_ref[:, at] = state[1]

            @pl.when(half == side)
            def _():
                store(absorb(kv_ref[side, 0, :, kv], kv_ref[side, 1, :, kv], diagonal, qt, None))

            @pl.when(half != side)
            def _():
                both = [jnp.concatenate([kv_ref[1 - side, i, :, kv], kv_ref[side, i, :, kv]], axis=0) for i in range(2)]
                store(absorb(both[0], both[1], jnp.concatenate([earlier, diagonal], axis=0), qt, None))

            return 0

        lax.fori_loop(0, kv_heads, one_group, 0)

    tokens(1, q_far_ref)
    fetch.wait()
    tokens(0, q_near_ref)


def span_steps(place_ref, lengths_ref, kv_ref, qt_ref, number, side, load, store):
    rows = kv_ref.shape[2]
    kv_heads = kv_ref.shape[3] // HD
    width = qt_ref.shape[1] // (2 * kv_heads)
    first = place_ref[side]
    key_starts = place_ref[3 + 2 * number], place_ref[4 + 2 * number]
    lo_first, lo_last = doc_starts(lengths_ref, first, first + rows - 1)
    needed = jnp.maximum(key_starts[0], key_starts[1]) + rows > lo_first
    whole = jnp.minimum(key_starts[0], key_starts[1]) >= lo_last

    def work(masked):
        allowed = None
        if masked:
            allowed = positions(key_starts, rows) >= doc_start_rows(lengths_ref, first, 2 * rows, rows)

        def one_group(g, _):
            kv = lanes(g, HD)
            keys, values = (jnp.concatenate([kv_ref[0, i, :, kv], kv_ref[1, i, :, kv]], axis=0) for i in range(2))
            qt = qt_ref[:, lanes(side * kv_heads + g, width)]
            store(g, absorb(keys, values, allowed, qt, load(g)))
            return 0

        lax.fori_loop(0, kv_heads, one_group, 0)

    pl.when(whole)(lambda: work(False))
    pl.when(needed & jnp.logical_not(whole))(lambda: work(True))
    return needed


def span_kernel(place_ref, lengths_ref, kv_ref, qt_ref, max_in, acc_in, max_ref, acc_ref, *, number):
    del max_in, acc_in
    kv_heads = kv_ref.shape[3] // HD
    width = qt_ref.shape[1] // (2 * kv_heads)
    for side in range(2):

        def load(g):
            at = lanes(side * kv_heads + g, width)
            return max_ref[:1, at], acc_ref[:, at]

        def store(g, state):
            at = lanes(side * kv_heads + g, width)
            max_ref[:, at] = jnp.broadcast_to(state[0], (8, width))
            acc_ref[:, at] = state[1]

        span_steps(place_ref, lengths_ref, kv_ref, qt_ref, number, side, load, store)


def last_kernel(place_ref, lengths_ref, kv_ref, qt_ref, max_ref, acc_ref, out_ref, *refs, number, side):
    rows = kv_ref.shape[2]
    kv_heads = kv_ref.shape[3] // HD
    width = qt_ref.shape[1] // (2 * kv_heads)
    group_size = width // rows
    out = out_ref
    if refs:
        out, sem = refs

    def load(g):
        at = lanes(side * kv_heads + g, width)
        return max_ref[:1, at], acc_ref[:, at]

    def finish(g, state):
        acc = state[1]
        finished = (acc[:HD] * (1.0 / acc[HD : HD + 1])).astype(out.dtype)
        out[:, lanes(g, group_size * HD)] = turned(finished, group_size)

    needed = span_steps(place_ref, lengths_ref, kv_ref, qt_ref, number, side, load, finish)

    @pl.when(jnp.logical_not(needed))
    def _():
        def one_group(g, _):
            finish(g, load(g))
            return 0

        lax.fori_loop(0, kv_heads, one_group, 0)

    if refs:
        copy = pltpu.make_async_copy(out, out_ref.at[:, lanes(place_ref[2], out.shape[1])], sem)
        copy.start()
        copy.wait()


def join_kernel(place_ref, far_ref, out_in, out_ref, sem):
    del out_in
    copy = pltpu.make_async_copy(far_ref, out_ref.at[:, lanes(1 - place_ref[2], far_ref.shape[1])], sem)
    copy.start()
    copy.wait()


def per_device(queries, keys, values, doc_lengths):
    rows, all_heads = queries.shape
    half_heads = all_heads // 2
    head_rows = (all_heads // HD) * rows
    half, span = lax.axis_index("head"), lax.axis_index("ctx")
    cores = lax.axis_size("head")
    place_in_group = lax.rem(span, REACH)

    def source(partner):
        from_place = place_in_group ^ partner
        return span - place_in_group + from_place - jnp.where(from_place > place_in_group, REACH, 0)

    mine = [jnp.where(half == 0, PARTNER[0][turn], PARTNER[1][turn]) for turn in range(2)]
    parts = [(span * cores + half) * rows, (span * cores + 1 - half) * rows, half]
    for origin in (span - REACH, source(REACH - 1), source(mine[0]), source(mine[1])):
        parts += [(origin * cores + half) * rows, (origin * cores + 1 - half) * rows]
    place = jnp.stack(parts).astype(jnp.int32)

    vmem = pl.BlockSpec(memory_space=pltpu.VMEM)
    smem = pl.BlockSpec(memory_space=pltpu.SMEM)
    anywhere = pl.BlockSpec(memory_space=pl.ANY)
    qt_shape = jax.ShapeDtypeStruct((HD, head_rows), queries.dtype)
    max_shape = jax.ShapeDtypeStruct((8, head_rows), jnp.float32)
    acc_shape = jax.ShapeDtypeStruct((HD + SUM_ROWS, head_rows), jnp.float32)
    side_shape = jax.ShapeDtypeStruct((rows, half_heads), queries.dtype)
    common = dict(
        compiler_params=pltpu.CompilerParams(vmem_limit_bytes=24 * 1024 * 1024),
        cost_estimate=pl.CostEstimate(flops=0, bytes_accessed=0, transcendentals=0),
    )

    def heads_of(array, core):
        width = array.shape[1] // 2
        return lax.dynamic_slice_in_dim(array, core * width, width, 1)

    given = to_other_core(jnp.stack([heads_of(keys, 1 - half), heads_of(values, 1 - half)]))
    own = jnp.stack([jnp.stack([heads_of(keys, half), heads_of(values, half)]), given])
    behind = to_next_group(own)
    opposite = to_opposite(own)
    q_far = to_other_core(heads_of(queries, 1 - half))

    qt, row_max, acc = pl.pallas_call(
        own_kernel,
        in_specs=[smem, smem, anywhere, vmem, vmem],
        out_specs=(vmem, vmem, vmem),
        out_shape=(qt_shape, max_shape, acc_shape),
        scratch_shapes=[pltpu.VMEM((rows, half_heads), queries.dtype), pltpu.SemaphoreType.DMA],
        name="attend_own",
        **common,
    )(place, doc_lengths, queries, q_far, own)

    def attend(kv, row_max, acc, number):
        return pl.pallas_call(
            functools.partial(span_kernel, number=number),
            in_specs=[smem, smem] + [vmem] * 4,
            out_specs=(vmem, vmem),
            out_shape=(max_shape, acc_shape),
            input_output_aliases={4: 0, 5: 1},
            name="attend_span",
            **common,
        )(place, doc_lengths, kv, qt, row_max, acc)

    behind, acc = lax.optimization_barrier((behind, acc))
    exchanged = []
    for turn in range(2):
        send = jnp.where((place_in_group ^ mine[turn]) > place_in_group, own, behind)
        exchanged.append(in_group(send, turn))
    row_max, acc = attend(behind, row_max, acc, 0)
    row_max, acc = attend(opposite, row_max, acc, 1)
    row_max, acc = attend(exchanged[0], row_max, acc, 2)

    last_args = (place, doc_lengths, exchanged[1], qt, row_max, acc)
    out_far = pl.pallas_call(
        functools.partial(last_kernel, number=3, side=1),
        in_specs=[smem, smem] + [vmem] * 4,
        out_specs=vmem,
        out_shape=side_shape,
        name="attend_last_far",
        **common,
    )(*last_args)
    out = pl.pallas_call(
        functools.partial(last_kernel, number=3, side=0),
        in_specs=[smem, smem] + [vmem] * 4,
        out_specs=anywhere,
        out_shape=jax.ShapeDtypeStruct(queries.shape, queries.dtype),
        scratch_shapes=[pltpu.VMEM((rows, half_heads), queries.dtype), pltpu.SemaphoreType.DMA],
        name="attend_last_near",
        **common,
    )(*last_args)
    return pl.pallas_call(
        join_kernel,
        in_specs=[smem, vmem, anywhere],
        out_specs=anywhere,
        out_shape=jax.ShapeDtypeStruct(queries.shape, queries.dtype),
        input_output_aliases={2: 0},
        scratch_shapes=[pltpu.SemaphoreType.DMA],
        name="join_heads",
        **common,
    )(place, to_other_core(out_far), out)


def solution(mesh):
    placed = P(AXES, None)
    return jax.shard_map(
        per_device, mesh=mesh, in_specs=(placed, placed, placed, P()), out_specs=placed, check_vma=False
    )
```

time: 63 us -> 62.2 us (0.987)
  the two profiles are of different devices: /device:TPU:8 before, /device:TPU:19 now
where the time goes in v5:
time: 62.2 us; the launch traced here: 61.9 us
  Pallas kernels  35.5 us (57%)
  waiting for transfers between devices  14 us (23%)
  starting transfers between devices  8.85 us (14%)
  local copies, waits for them, and re-layouts  3.19 us (5%)
    pallas_call x3, Pallas kernels, attend(): pl.pallas_call(functools.partial(span_kernel, number=number), in_specs=[s...  18.3 us
    pallas_call x1, Pallas kernels, per_device(): pl.pallas_call(own_kernel, in_specs=[smem, smem, anywhere, vmem, vmem], o...  7.06 us
    ppermute x2, waiting for transfers between devices, in_group(): return lax.ppermute(block, AXES, pairs)  5.76 us
    pallas_call x1, Pallas kernels, per_device(): pl.pallas_call(functools.partial(last_kernel, number=3, side=0), in_specs...  4.74 us
    ppermute x1, waiting for transfers between devices, to_opposite(): return lax.ppermute(block, AXES, pairs)  4.46 us
    pallas_call x1, Pallas kernels, per_device(): pl.pallas_call(functools.partial(last_kernel, number=3, side=1), in_specs...  3.9 us
    ppermute x1, starting transfers between devices, to_opposite(): return lax.ppermute(block, AXES, pairs)  3.25 us
    ppermute x1, starting transfers between devices, to_next_group(): return lax.ppermute(block, AXES, pairs)  3.2 us
  transfers between devices with their start and end apart: 7, of which 4 were waited for; matrix products, arithmetic and copies ran while one was open for 0% of the time, Pallas kernels for 49%

profile of v5, /device:TPU:19, one launch (start us, length us, event | category | flops | bytes accessed | tf_op | source)
XLA Modules:
  0.0 61.9 jit_solution(750204508290057239)
XLA Ops:
  0.0 0.0 copy-start.4
  0.0 0.0 copy-start.5
  0.0 2.3 %constant_dynamic-slice_fusion = bf16[128,4096]{1,0:T(8,128)(2,1)} fusion(bf16[128,8192]{1,0:T(8,128)(2,1)} %q_ref.1, s32[]{:T(128)S(6)} %select_n.49), kind=kLoop, calls=%fused_computation.9 | loop fusion | bytes 2097156 | tf_op jit(solution)/shard_map/dynamic_slice | solution.py:270
  2.3 0.0 copy-start
  2.4 0.0 copy-start.1
  2.4 0.7 %collective-permute-start.2 = (bf16[128,4096]{1,0:T(8,128)(2,1)}, bf16[128,4096]{1,0:T(8,128)(2,1)}, u32[]{:S(2)}, u32[]{:S(2)}) collective-permute-start(bf16[128,4096]{1,0:T(8,128)(2,1)} %constant_dynamic-slice_fusion), channel_id=1, source_target_pairs={{0,1},{1,0},{2,3},{3,2},{4,5},{5,4},{6,7},{7,6},{8,9},{9,8},{10,11... | collective-permute-start | bytes 3145736 | tf_op jit(solution)/shard_map/ppermute | solution.py:49
  3.0 0.0 copy-done.4
  3.0 0.0 copy-done.5
  3.1 0.1 collective-permute-start
  3.2 2.5 %collective-permute-done = bf16[2,128,512]{2,1,0:T(8,128)(2,1)S(1)} collective-permute-done((bf16[2,128,512]{2,1,0:T(8,128)(2,1)S(1)}, bf16[2,128,512]{2,1,0:T(8,128)(2,1)S(1)}, u32[]{:S(2)}, u32[]{:S(2)}) %collective-permute-start) | collective-permute-done | bytes 262176 | tf_op jit(solution)/shard_map/ppermute | solution.py:49
  5.7 0.0 copy-start.2
  5.7 0.7 %copy-done.2 = bf16[2,128,512]{2,1,0:T(8,128)(2,1)} copy-done((bf16[2,128,512]{2,1,0:T(8,128)(2,1)}, bf16[2,128,512]{2,1,0:T(8,128)(2,1)S(1)}, u32[]{:S(2)}) %copy-start.2) | copy-done | bytes 262168
  6.4 0.1 pad_maximum_fusion.kv_ref
  6.5 3.2 %collective-permute-start.1 = (bf16[2,2,128,512]{3,2,1,0:T(8,128)(2,1)S(1)}, bf16[2,2,128,512]{3,2,1,0:T(8,128)(2,1)S(1)}, u32[]{:S(2)}, u32[]{:S(2)}) collective-permute-start(bf16[2,2,128,512]{3,2,1,0:T(8,128)(2,1)S(1)} %pad_maximum_fusion.kv_ref), channel_id=1, source_target_pairs={{0,8},{1,9},{2,10},{3,11},{4,12},{5,13},{6,14},{7,15},{8,16},{9,17... | collective-permute-start | bytes 1572872 | tf_op jit(solution)/shard_map/ppermute | solution.py:23
  9.7 0.1 stack.74.place_ref
  9.8 0.0 copy-start.3
  9.8 3.3 %collective-permute-start.5 = (bf16[2,2,128,512]{3,2,1,0:T(8,128)(2,1)S(1)}, bf16[2,2,128,512]{3,2,1,0:T(8,128)(2,1)S(1)}, u32[]{:S(2)}, u32[]{:S(2)}) collective-permute-start(bf16[2,2,128,512]{3,2,1,0:T(8,128)(2,1)S(1)} %pad_maximum_fusion.kv_ref), channel_id=1, source_target_pairs={{0,6},{1,7},{2,4},{3,5},{4,10},{5,11},{6,8},{7,9},{8,14},{9,15},{1... | collective-permute-start | bytes 1572872 | tf_op jit(solution)/shard_map/ppermute | solution.py:35
  13.1 0.0 collective-permute-done.2.q_far_ref
  13.1 0.0 copy-done
  13.1 0.0 copy-done.1
  13.1 7.1 %attend_own.1 = (bf16[128,8192]{1,0:T(8,128)(2,1)S(1)}, f32[8,8192]{1,0:T(8,128)S(1)}, f32[144,8192]{1,0:T(8,128)S(1)}) custom-call(s32[11]{0:T(128)S(1)} %stack.74.place_ref, s32[12]{0:T(128)S(1)} %copy-done.1, bf16[128,8192]{1,0:T(8,128)(2,1)S(1)} %copy-done, bf16[128,4096]{1,0:T(8,128)(2,1)} %collective-permute-done.2.q_far_ref, ...), custom_call_target="tpu_custom_call" | custom-call | tf_op jit(solution)/shard_map/attend_own/pallas_call | solution.py:278
  20.2 1.3 %collective-permute-done.1.kv_ref = bf16[2,2,128,512]{3,2,1,0:T(8,128)(2,1)S(1)} collective-permute-done((bf16[2,2,128,512]{3,2,1,0:T(8,128)(2,1)S(1)}, bf16[2,2,128,512]{3,2,1,0:T(8,128)(2,1)S(1)}, u32[]{:S(2)}, u32[]{:S(2)}) %collective-permute-start.1) | collective-permute-done | bytes 524320 | tf_op jit(solution)/shard_map/ppermute | solution.py:23
  21.5 0.0 copy-done.3
  21.5 0.1 broadcast_select_fusion
  21.6 1.3 %collective-permute-start.4 = (bf16[2,2,128,512]{3,2,1,0:T(8,128)(2,1)S(1)}, bf16[2,2,128,512]{3,2,1,0:T(8,128)(2,1)S(1)}, u32[]{:S(2)}, u32[]{:S(2)}) collective-permute-start(bf16[2,2,128,512]{3,2,1,0:T(8,128)(2,1)S(1)} %get-tuple-element.27), channel_id=1, source_target_pairs={{0,2},{1,5},{2,0},{3,7},{4,6},{5,1},{6,4},{7,3},{8,10},{9,13},{10,... | collective-permute-start | bytes 1572872 | tf_op jit(solution)/shard_map/ppermute | solution.py:44
  22.9 0.3 collective-permute-start.3
  23.1 6.1 %attend_span.3 = (f32[8,8192]{1,0:T(8,128)S(1)}, f32[144,8192]{1,0:T(8,128)S(1)}) custom-call(s32[11]{0:T(128)S(1)} %stack.74.place_ref, s32[12]{0:T(128)S(1)} %copy-done.1, bf16[2,2,128,512]{3,2,1,0:T(8,128)(2,1)S(1)} %collective-permute-done.1.kv_ref, ...), custom_call_target="tpu_custom_call", output_to_operand_aliasing={{0}: (4, {}), {1}: (5, {})} | custom-call | tf_op jit(solution)/shard_map/attend_span/pallas_call | solution.py:289
  29.2 4.5 %collective-permute-done.5.kv_ref = bf16[2,2,128,512]{3,2,1,0:T(8,128)(2,1)S(1)} collective-permute-done((bf16[2,2,128,512]{3,2,1,0:T(8,128)(2,1)S(1)}, bf16[2,2,128,512]{3,2,1,0:T(8,128)(2,1)S(1)}, u32[]{:S(2)}, u32[]{:S(2)}) %collective-permute-start.5) | collective-permute-done | bytes 524320 | tf_op jit(solution)/shard_map/ppermute | solution.py:35
  33.7 6.1 %attend_span.4 = (f32[8,8192]{1,0:T(8,128)S(1)}, f32[144,8192]{1,0:T(8,128)S(1)}) custom-call(s32[11]{0:T(128)S(1)} %stack.74.place_ref, s32[12]{0:T(128)S(1)} %copy-done.1, bf16[2,2,128,512]{3,2,1,0:T(8,128)(2,1)S(1)} %collective-permute-done.5.kv_ref, ...), custom_call_target="tpu_custom_call", output_to_operand_aliasing={{0}: (4, {}), {1}: (5, {})} | custom-call | tf_op jit(solution)/shard_map/attend_span/pallas_call | solution.py:289
  39.8 5.8 %collective-permute-done.4.kv_ref = bf16[2,2,128,512]{3,2,1,0:T(8,128)(2,1)S(1)} collective-permute-done((bf16[2,2,128,512]{3,2,1,0:T(8,128)(2,1)S(1)}, bf16[2,2,128,512]{3,2,1,0:T(8,128)(2,1)S(1)}, u32[]{:S(2)}, u32[]{:S(2)}) %collective-permute-start.4) | collective-permute-done | bytes 524320 | tf_op jit(solution)/shard_map/ppermute | solution.py:44
  45.5 6.1 %attend_span.5 = (f32[8,8192]{1,0:T(8,128)S(1)}, f32[144,8192]{1,0:T(8,128)S(1)}) custom-call(s32[11]{0:T(128)S(1)} %stack.74.place_ref, s32[12]{0:T(128)S(1)} %copy-done.1, bf16[2,2,128,512]{3,2,1,0:T(8,128)(2,1)S(1)} %collective-permute-done.4.kv_ref, ...), custom_call_target="tpu_custom_call", output_to_operand_aliasing={{0}: (4, {}), {1}: (5, {})} | custom-call | tf_op jit(solution)/shard_map/attend_span/pallas_call | solution.py:289
  51.6 0.0 collective-permute-done.3.kv_ref
  51.6 3.9 %attend_last_far.1 = bf16[128,4096]{1,0:T(8,128)(2,1)S(1)} custom-call(s32[11]{0:T(128)S(1)} %stack.74.place_ref, s32[12]{0:T(128)S(1)} %copy-done.1, bf16[2,2,128,512]{3,2,1,0:T(8,128)(2,1)S(1)} %collective-permute-done.3.kv_ref, bf16[128,8192]{1,0:T(8,128)(2,1)S(1)} %get-tuple-element.18.qt_ref, f32[8,8192]{1,0:T(8,128)S(1)} %get-tuple-element.25.max_ref, ...), custom_call_target="tpu_custom_call" | custom-call | tf_op jit(solution)/shard_map/attend_last_far/pallas_call | solution.py:309
  55.6 0.1 collective-permute-start.6
  55.6 4.7 %attend_last_near.1.out_in = bf16[128,8192]{1,0:T(8,128)(2,1)} custom-call(s32[11]{0:T(128)S(1)} %stack.74.place_ref, s32[12]{0:T(128)S(1)} %copy-done.1, bf16[2,2,128,512]{3,2,1,0:T(8,128)(2,1)S(1)} %collective-permute-done.3.kv_ref, bf16[128,8192]{1,0:T(8,128)(2,1)S(1)} %get-tuple-element.18.qt_ref, f32[8,8192]{1,0:T(8,128)S(1)} %get-tuple-element.25.max_ref, ...), custom_call_target="tpu_custom_call" | custom-call | tf_op jit(solution)/shard_map/attend_last_near/pallas_call | solution.py:317
  60.4 0.0 collective-permute-done.6.far_ref
  60.4 1.5 %join_heads.1 = bf16[128,8192]{1,0:T(8,128)(2,1)} custom-call(s32[11]{0:T(128)S(1)} %stack.74.place_ref, bf16[128,4096]{1,0:T(8,128)(2,1)S(1)} %collective-permute-done.6.far_ref, bf16[128,8192]{1,0:T(8,128)(2,1)} %attend_last_near.1.out_in), custom_call_target="tpu_custom_call", output_to_operand_aliasing={{}: (2, {})} | custom-call | tf_op jit(solution)/shard_map/join_heads/pallas_call | solution.py:326
  (3 shorter events, 0.1 us)
Async XLA Ops:
  0.0 3.0 %copy-start.4 = (bf16[128,1024]{1,0:T(8,128)(2,1)S(1)}, bf16[128,1024]{1,0:T(8,128)(2,1)}, u32[]{:S(2)}) copy-start(bf16[128,1024]{1,0:T(8,128)(2,1)} %param.6) | copy-start | bytes 786436
  0.0 3.0 %copy-start.5 = (bf16[128,1024]{1,0:T(8,128)(2,1)S(1)}, bf16[128,1024]{1,0:T(8,128)(2,1)}, u32[]{:S(2)}) copy-start(bf16[128,1024]{1,0:T(8,128)(2,1)} %param.5) | copy-start | bytes 786436
  2.3 10.7 %copy-start = (bf16[128,8192]{1,0:T(8,128)(2,1)S(1)}, bf16[128,8192]{1,0:T(8,128)(2,1)}, u32[]{:S(2)}) copy-start(bf16[128,8192]{1,0:T(8,128)(2,1)} %q_ref.1) | copy-start | bytes 6291460
  2.4 10.7 %copy-start.1 = (s32[12]{0:T(128)S(1)}, s32[12]{0:T(128)}, u32[]{:S(2)}) copy-start(s32[12]{0:T(128)} %lengths_ref.11) | copy-start | bytes 148
  2.4 10.7 %collective-permute-start.2 = (bf16[128,4096]{1,0:T(8,128)(2,1)}, bf16[128,4096]{1,0:T(8,128)(2,1)}, u32[]{:S(2)}, u32[]{:S(2)}) collective-permute-start(bf16[128,4096]{1,0:T(8,128)(2,1)} %constant_dynamic-slice_fusion), channel_id=1, source_target_pairs={{0,1},{1,0},{2,3},{3,2},{4,5},{5,4},{6,7},{7,6},{8,9},{9,8},{10,11... | collective-permute-start | bytes 3145736 | tf_op jit(solution)/shard_map/ppermute | solution.py:49
  3.1 2.6 %collective-permute-start = (bf16[2,128,512]{2,1,0:T(8,128)(2,1)S(1)}, bf16[2,128,512]{2,1,0:T(8,128)(2,1)S(1)}, u32[]{:S(2)}, u32[]{:S(2)}) collective-permute-start(bf16[2,128,512]{2,1,0:T(8,128)(2,1)S(1)} %pad_maximum_fusion.1), channel_id=1, source_target_pairs={{0,1},{1,0},{2,3},{3,2},{4,5},{5,4},{6,7},{7,6},{8,9},{9,8},{10,11... | collective-permute-start | bytes 786440 | tf_op jit(solution)/shard_map/ppermute | solution.py:49
  5.7 0.7 %copy-start.2 = (bf16[2,128,512]{2,1,0:T(8,128)(2,1)}, bf16[2,128,512]{2,1,0:T(8,128)(2,1)S(1)}, u32[]{:S(2)}) copy-start(bf16[2,128,512]{2,1,0:T(8,128)(2,1)S(1)} %collective-permute-done) | copy-start | bytes 786436
  6.5 15.0 %collective-permute-start.1 = (bf16[2,2,128,512]{3,2,1,0:T(8,128)(2,1)S(1)}, bf16[2,2,128,512]{3,2,1,0:T(8,128)(2,1)S(1)}, u32[]{:S(2)}, u32[]{:S(2)}) collective-permute-start(bf16[2,2,128,512]{3,2,1,0:T(8,128)(2,1)S(1)} %pad_maximum_fusion.kv_ref), channel_id=1, source_target_pairs={{0,8},{1,9},{2,10},{3,11},{4,12},{5,13},{6,14},{7,15},{8,16},{9,17... | collective-permute-start | bytes 1572872 | tf_op jit(solution)/shard_map/ppermute | solution.py:23
  9.8 11.7 %copy-start.3 = (bf16[2,128,512]{2,1,0:T(8,128)(2,1)S(1)}, bf16[2,128,512]{2,1,0:T(8,128)(2,1)}, u32[]{:S(2)}) copy-start(bf16[2,128,512]{2,1,0:T(8,128)(2,1)} %copy-done.2) | copy-start | bytes 786436
  9.8 23.9 %collective-permute-start.5 = (bf16[2,2,128,512]{3,2,1,0:T(8,128)(2,1)S(1)}, bf16[2,2,128,512]{3,2,1,0:T(8,128)(2,1)S(1)}, u32[]{:S(2)}, u32[]{:S(2)}) collective-permute-start(bf16[2,2,128,512]{3,2,1,0:T(8,128)(2,1)S(1)} %pad_maximum_fusion.kv_ref), channel_id=1, source_target_pairs={{0,6},{1,7},{2,4},{3,5},{4,10},{5,11},{6,8},{7,9},{8,14},{9,15},{1... | collective-permute-start | bytes 1572872 | tf_op jit(solution)/shard_map/ppermute | solution.py:35
  21.6 24.0 %collective-permute-start.4 = (bf16[2,2,128,512]{3,2,1,0:T(8,128)(2,1)S(1)}, bf16[2,2,128,512]{3,2,1,0:T(8,128)(2,1)S(1)}, u32[]{:S(2)}, u32[]{:S(2)}) collective-permute-start(bf16[2,2,128,512]{3,2,1,0:T(8,128)(2,1)S(1)} %get-tuple-element.27), channel_id=1, source_target_pairs={{0,2},{1,5},{2,0},{3,7},{4,6},{5,1},{6,4},{7,3},{8,10},{9,13},{10,... | collective-permute-start | bytes 1572872 | tf_op jit(solution)/shard_map/ppermute | solution.py:44
  22.9 28.8 %collective-permute-start.3 = (bf16[2,2,128,512]{3,2,1,0:T(8,128)(2,1)S(1)}, bf16[2,2,128,512]{3,2,1,0:T(8,128)(2,1)S(1)}, u32[]{:S(2)}, u32[]{:S(2)}) collective-permute-start(bf16[2,2,128,512]{3,2,1,0:T(8,128)(2,1)S(1)} %get-tuple-element.28), channel_id=1, source_target_pairs={{0,4},{1,3},{2,6},{3,1},{4,0},{5,7},{6,2},{7,5},{8,12},{9,11},{10,... | collective-permute-start | bytes 1572872 | tf_op jit(solution)/shard_map/ppermute | solution.py:44
  55.6 4.8 %collective-permute-start.6 = (bf16[128,4096]{1,0:T(8,128)(2,1)S(1)}, bf16[128,4096]{1,0:T(8,128)(2,1)S(1)}, u32[]{:S(2)}, u32[]{:S(2)}) collective-permute-start(bf16[128,4096]{1,0:T(8,128)(2,1)S(1)} %attend_last_far.1), channel_id=1, source_target_pairs={{0,1},{1,0},{2,3},{3,2},{4,5},{5,4},{6,7},{7,6},{8,9},{9,8},{10,11... | collective-permute-start | bytes 3145736 | tf_op jit(solution)/shard_map/ppermute | solution.py:49
